TPU v7x, 256 devices: a whole 4x4x8 slice. The times are simulated.
256 devices in a mesh: blk: 32 (over z_lo, y, core), col: 2 (over z_hi), rep: 4 (over x).
Axes of the slice: x: 4, y: 4, z: 8 (z_hi: 2, z_lo: 4; z = z_hi * 4 + z_lo), core: 2. Of those that a mesh axis runs over, the one named last changes fastest.
Arguments:
- feats: bfloat16 [65536, 256], P('blk', 'col'), may hold values from -6 to 6
- agg_feats: bfloat16 [65536, 256], P('blk', 'col'), may hold values from -6 to 6
- grad_out: bfloat16 [65536, 256], P('blk', 'col'), may hold values from -6 to 6
- w_self: bfloat16 [256, 256], P('col'), may hold values from -0.375 to 0.375
- w_neigh: bfloat16 [256, 256], P('col'), may hold values from -0.375 to 0.375
- degree: int32 [65536], P('blk'), may hold values from 1 to 64
- tile_vals: bfloat16 [32, 32, 40, 128, 128], P('blk', 'rep'), may hold values from 0 to 1
- tile_rows: int32 [32, 32, 40], P('blk', 'rep'), may hold values from 0 to 15
- tile_cols: int32 [32, 32, 40], P('blk', 'rep'), may hold values from 0 to 15
- tile_count: int32 [32, 32], P('blk', 'rep'), may hold values from 0 to 40, as said below
Outputs:
- grad_feats: bfloat16 [65536, 256], P('blk', 'col')
- grad_weight: float32 [2, 256, 256], P(None, 'col')
Inputs may be any that keep to these rules, and one draw needn't show every extreme that they name: `tile_count`: the tile slots of a pair at or past its count hold tiles that are not part of the graph.
All inputs are finite; a program needn't handle non-finite values.
Results may differ from a plain program's by a relative error of at most 0.0049.
Values may be sent and summed in bfloat16 or wider, within the bound.
No kernel may reach another device: no remote copies, remote signals or barrier semaphores. Data moves between devices by JAX's collectives and lax.ppermute only.
A program may use at most 128 MiB of HBM per device.

v0:
```python
import math

import jax
import jax.numpy as jnp
from jax import lax
from jax.sharding import PartitionSpec as P


def passed_along(block, axis, distance):
    devices = range(lax.axis_size(axis))
    route = [((i - distance) % len(devices), i) for i in devices]
    return lax.ppermute(block, axis, route)


def shards(
    feats, agg_feats, grad_out, w_self, w_neigh, degree, tile_vals, tile_rows, tile_cols, tile_count
):
    cotangent = lax.all_gather(grad_out, "col", axis=1, tiled=True)
    row_count, feature_width = feats.shape
    tile_size = tile_vals.shape[3]
    tiles_dev = row_count // tile_size
    cycle_steps = tile_vals.shape[1]
    slot_count = tile_vals.shape[2]
    contract = (((1,), (1,)), ((), ()))
    scaled = (
        lax.dot_general(cotangent, w_neigh, contract, preferred_element_type=jnp.float32)
        / degree.astype(jnp.float32)[:, None]
    ).astype(jnp.bfloat16)
    gradient_panel = scaled.reshape(tiles_dev, tile_size, feature_width)
    groups = lax.axis_size("rep")
    member = lax.axis_index("rep")
    for bit_index in range(groups.bit_length() - 1):
        arrived = passed_along(gradient_panel, "blk", cycle_steps << bit_index)
        gradient_panel = jnp.where(member >> bit_index & 1 == 1, arrived, gradient_panel)
    live_slots = jnp.arange(slot_count)

    def contribute(accumulated, current, cycle_step):
        edge_values = lax.dynamic_index_in_dim(tile_vals[0], cycle_step, 0, keepdims=False)
        sources = lax.dynamic_index_in_dim(tile_rows[0], cycle_step, 0, keepdims=False)
        targets = lax.dynamic_index_in_dim(tile_cols[0], cycle_step, 0, keepdims=False)
        live_count = lax.dynamic_index_in_dim(tile_count[0], cycle_step, 0, keepdims=False)
        picked = jnp.take(current, sources, axis=0)
        product = jnp.einsum(
            "tab,taf->tbf", edge_values, picked, preferred_element_type=jnp.float32
        )
        product = jnp.where(
            (live_slots < live_count)[:, None, None], product, jnp.zeros_like(product)
        )
        return accumulated.at[targets].add(product)

    accumulated = contribute(
        jnp.zeros((tiles_dev, tile_size, feature_width), jnp.float32), gradient_panel, 0
    )

    def advance(cycle_step, carry):
        running, current = carry
        current = passed_along(current, "blk", 1)
        return (contribute(running, current, cycle_step), current)

    accumulated, gradient_panel = lax.fori_loop(
        1, cycle_steps, advance, (accumulated, gradient_panel)
    )
    neighbour = lax.psum(accumulated.reshape(row_count, feature_width), "rep")
    self_term = lax.dot_general(cotangent, w_self, contract, preferred_element_type=jnp.float32)
    grad_feats = (self_term + neighbour).astype(jnp.bfloat16)
    row_contract = (((0,), (0,)), ((), ()))
    node_count = row_count * lax.axis_size("blk")
    partial_sums = jnp.stack(
        [
            lax.dot_general(feats, cotangent, row_contract, preferred_element_type=jnp.float32),
            lax.dot_general(agg_feats, cotangent, row_contract, preferred_element_type=jnp.float32),
        ]
    )
    summed = lax.psum(partial_sums, "blk")
    grad_weight = summed * (1.0 / math.sqrt(node_count))
    return (grad_feats, grad_weight)


def solution(mesh):
    placed = (
        P("blk", "col"),
        P("blk", "col"),
        P("blk", "col"),
        P("col", None),
        P("col", None),
        P("blk"),
        P("blk", "rep", None, None, None),
        P("blk", "rep", None),
        P("blk", "rep", None),
        P("blk", "rep"),
    )
    return jax.shard_map(
        shards,
        mesh=mesh,
        in_specs=placed,
        out_specs=(P("blk", "col"), P(None, "col", None)),
        check_vma=False,
    )
```

profile of v0, /device:TPU:32, one launch (start us, length us, event | category | flops | bytes accessed | tf_op | source)
XLA Modules:
  0.0 407.2 jit_solution(8778680055499163996)
XLA Ops:
  8.7 44.5 %all-gather.2.cloned.1.call-done = bf16[2048,256]{1,0:T(8,128)(2,1)} async-done(((bf16[2048,128]{1,0:T(8,128)(2,1)}), bf16[2048,256]{1,0:T(8,128)(2,1)}) %all-gather.2.cloned.1.call-update) | async-done | bytes 1048592 | tf_op jit(solution)/shard_map/all_gather | solution.py:18
  56.7 12.0 %collective-permute-done.1 = bf16[16,128,128]{2,1,0:T(8,128)(2,1)S(1)} collective-permute-done((bf16[16,128,128]{2,1,0:T(8,128)(2,1)S(1)}, bf16[16,128,128]{2,1,0:T(8,128)(2,1)S(1)}, u32[]{:S(2)}, u32[]{:S(2)}) %collective-permute-start.1) | collective-permute-done | bytes 524320 | tf_op jit(solution)/shard_map/ppermute | solution.py:12
  71.9 20.0 %collective-permute-done.2 = bf16[16,128,128]{2,1,0:T(8,128)(2,1)S(1)} collective-permute-done((bf16[16,128,128]{2,1,0:T(8,128)(2,1)S(1)}, bf16[16,128,128]{2,1,0:T(8,128)(2,1)S(1)}, u32[]{:S(2)}, u32[]{:S(2)}) %collective-permute-start.2) | collective-permute-done | bytes 524320 | tf_op jit(solution)/shard_map/ppermute | solution.py:12
  91.9 1.9 gather_fusion.1
  93.8 2.5 select_bitcast_fusion
  96.3 2.1 copy.13
  98.5 6.6 %scatter_fusion.1 = f32[16,128,128]{2,1,0:T(8,128)S(1)} fusion(f32[16,128,128]{2,1,0:T(8,128)S(1)} %broadcast_in_dim.47, s32[40]{0:T(128)S(1)} %fusion.19, f32[40,128,128]{2,1,0:T(8,128)} %copy.13), kind=kCustom, calls=%fused_computation.3 | custom fusion | flops 655360 | bytes 7864480 | tf_op jit(solution)/shard_map/scatter-add | solution.py:49
  105.1 154.4 %while.18 = (s32[]{:T(128)}, f32[16,128,128]{2,1,0:T(8,128)S(1)}, bf16[16,128,128]{2,1,0:T(8,128)(2,1)S(1)}, s32[1,8,40]{2,1,0:T(8,128)}, s32[1,8]{1,0:T(1,128)S...) while((s32[]{:T(128)}, f32[16,128,128]{2,1,0:T(8,128)S(1)}, ...), condition=%wide.region_3.5_spmd.clone, body=%wide.region_1.4_spmd.clone.sunk | while | flops 169739664 | bytes 18879956 | solution.py:60
  107.8 9.7 %collective-permute-done = bf16[16,128,128]{2,1,0:T(8,128)(2,1)S(1)} collective-permute-done((bf16[16,128,128]{2,1,0:T(8,128)(2,1)S(1)}, bf16[16,128,128]{2,1,0:T(8,128)(2,1)S(1)}, u32[]{:S(2)}, u32[]{:S(2)}) %collective-permute-start) | collective-permute-done | bytes 524320 | tf_op jit(solution)/shard_map/while/body/eval_jaxpr/ppermute | solution.py:12
  118.4 3.6 convolution_select_fusion.2
  121.9 6.5 %scatter_fusion = f32[16,128,128]{2,1,0:T(8,128)S(1)} fusion(f32[16,128,128]{2,1,0:T(8,128)S(1)} %get-tuple-element.304, s32[40]{0:T(128)S(1)} %fusion.34, f32[40,128,128]{2,1,0:T(8,128)} %convolution_select_fusion.2), kind=kCustom, calls=%fused_computation.2.clone.clone.1 | custom fusion | flops 655360 | bytes 7864480 | tf_op jit(solution)/shard_map/while/body/eval_jaxpr/scatter-add | solution.py:49
  131.3 8.2 %collective-permute-done = bf16[16,128,128]{2,1,0:T(8,128)(2,1)S(1)} collective-permute-done((bf16[16,128,128]{2,1,0:T(8,128)(2,1)S(1)}, bf16[16,128,128]{2,1,0:T(8,128)(2,1)S(1)}, u32[]{:S(2)}, u32[]{:S(2)}) %collective-permute-start) | collective-permute-done | bytes 524320 | tf_op jit(solution)/shard_map/while/body/eval_jaxpr/ppermute | solution.py:12
  140.2 3.6 convolution_select_fusion.2
  143.8 6.5 %scatter_fusion = f32[16,128,128]{2,1,0:T(8,128)S(1)} fusion(f32[16,128,128]{2,1,0:T(8,128)S(1)} %get-tuple-element.304, s32[40]{0:T(128)S(1)} %fusion.34, f32[40,128,128]{2,1,0:T(8,128)} %convolution_select_fusion.2), kind=kCustom, calls=%fused_computation.2.clone.clone.1 | custom fusion | flops 655360 | bytes 7864480 | tf_op jit(solution)/shard_map/while/body/eval_jaxpr/scatter-add | solution.py:49
  153.1 8.1 %collective-permute-done = bf16[16,128,128]{2,1,0:T(8,128)(2,1)S(1)} collective-permute-done((bf16[16,128,128]{2,1,0:T(8,128)(2,1)S(1)}, bf16[16,128,128]{2,1,0:T(8,128)(2,1)S(1)}, u32[]{:S(2)}, u32[]{:S(2)}) %collective-permute-start) | collective-permute-done | bytes 524320 | tf_op jit(solution)/shard_map/while/body/eval_jaxpr/ppermute | solution.py:12
  162.1 3.6 convolution_select_fusion.2
  165.6 6.5 %scatter_fusion = f32[16,128,128]{2,1,0:T(8,128)S(1)} fusion(f32[16,128,128]{2,1,0:T(8,128)S(1)} %get-tuple-element.304, s32[40]{0:T(128)S(1)} %fusion.34, f32[40,128,128]{2,1,0:T(8,128)} %convolution_select_fusion.2), kind=kCustom, calls=%fused_computation.2.clone.clone.1 | custom fusion | flops 655360 | bytes 7864480 | tf_op jit(solution)/shard_map/while/body/eval_jaxpr/scatter-add | solution.py:49
  175.0 8.1 %collective-permute-done = bf16[16,128,128]{2,1,0:T(8,128)(2,1)S(1)} collective-permute-done((bf16[16,128,128]{2,1,0:T(8,128)(2,1)S(1)}, bf16[16,128,128]{2,1,0:T(8,128)(2,1)S(1)}, u32[]{:S(2)}, u32[]{:S(2)}) %collective-permute-start) | collective-permute-done | bytes 524320 | tf_op jit(solution)/shard_map/while/body/eval_jaxpr/ppermute | solution.py:12
  183.9 3.6 convolution_select_fusion.2
  187.5 6.5 %scatter_fusion = f32[16,128,128]{2,1,0:T(8,128)S(1)} fusion(f32[16,128,128]{2,1,0:T(8,128)S(1)} %get-tuple-element.304, s32[40]{0:T(128)S(1)} %fusion.34, f32[40,128,128]{2,1,0:T(8,128)} %convolution_select_fusion.2), kind=kCustom, calls=%fused_computation.2.clone.clone.1 | custom fusion | flops 655360 | bytes 7864480 | tf_op jit(solution)/shard_map/while/body/eval_jaxpr/scatter-add | solution.py:49
  196.8 8.1 %collective-permute-done = bf16[16,128,128]{2,1,0:T(8,128)(2,1)S(1)} collective-permute-done((bf16[16,128,128]{2,1,0:T(8,128)(2,1)S(1)}, bf16[16,128,128]{2,1,0:T(8,128)(2,1)S(1)}, u32[]{:S(2)}, u32[]{:S(2)}) %collective-permute-start) | collective-permute-done | bytes 524320 | tf_op jit(solution)/shard_map/while/body/eval_jaxpr/ppermute | solution.py:12
  205.7 3.6 convolution_select_fusion.2
  209.2 6.5 %scatter_fusion = f32[16,128,128]{2,1,0:T(8,128)S(1)} fusion(f32[16,128,128]{2,1,0:T(8,128)S(1)} %get-tuple-element.304, s32[40]{0:T(128)S(1)} %fusion.34, f32[40,128,128]{2,1,0:T(8,128)} %convolution_select_fusion.2), kind=kCustom, calls=%fused_computation.2.clone.clone.1 | custom fusion | flops 655360 | bytes 7864480 | tf_op jit(solution)/shard_map/while/body/eval_jaxpr/scatter-add | solution.py:49
  218.6 8.1 %collective-permute-done = bf16[16,128,128]{2,1,0:T(8,128)(2,1)S(1)} collective-permute-done((bf16[16,128,128]{2,1,0:T(8,128)(2,1)S(1)}, bf16[16,128,128]{2,1,0:T(8,128)(2,1)S(1)}, u32[]{:S(2)}, u32[]{:S(2)}) %collective-permute-start) | collective-permute-done | bytes 524320 | tf_op jit(solution)/shard_map/while/body/eval_jaxpr/ppermute | solution.py:12
  227.5 3.6 convolution_select_fusion.2
  231.0 6.5 %scatter_fusion = f32[16,128,128]{2,1,0:T(8,128)S(1)} fusion(f32[16,128,128]{2,1,0:T(8,128)S(1)} %get-tuple-element.304, s32[40]{0:T(128)S(1)} %fusion.34, f32[40,128,128]{2,1,0:T(8,128)} %convolution_select_fusion.2), kind=kCustom, calls=%fused_computation.2.clone.clone.1 | custom fusion | flops 655360 | bytes 7864480 | tf_op jit(solution)/shard_map/while/body/eval_jaxpr/scatter-add | solution.py:49
  240.3 8.1 %collective-permute-done = bf16[16,128,128]{2,1,0:T(8,128)(2,1)S(1)} collective-permute-done((bf16[16,128,128]{2,1,0:T(8,128)(2,1)S(1)}, bf16[16,128,128]{2,1,0:T(8,128)(2,1)S(1)}, u32[]{:S(2)}, u32[]{:S(2)}) %collective-permute-start) | collective-permute-done | bytes 524320 | tf_op jit(solution)/shard_map/while/body/eval_jaxpr/ppermute | solution.py:12
  249.3 3.6 convolution_select_fusion.2
  252.8 6.5 %scatter_fusion = f32[16,128,128]{2,1,0:T(8,128)S(1)} fusion(f32[16,128,128]{2,1,0:T(8,128)S(1)} %get-tuple-element.304, s32[40]{0:T(128)S(1)} %fusion.34, f32[40,128,128]{2,1,0:T(8,128)} %convolution_select_fusion.2), kind=kCustom, calls=%fused_computation.2.clone.clone.1 | custom fusion | flops 655360 | bytes 7864480 | tf_op jit(solution)/shard_map/while/body/eval_jaxpr/scatter-add | solution.py:49
  260.5 72.4 %all-reduce.5.cloned.1.call-done = f32[2,128,256]{2,1,0:T(8,128)} async-done(((f32[2,128,256]{2,1,0:T(8,128)}), f32[2,128,256]{2,1,0:T(8,128)}) %all-reduce.5.cloned.1.call-update) | async-done | bytes 262160 | tf_op jit(solution)/shard_map/psum | solution.py:74
  334.5 63.8 %all-reduce.3.cloned.1.call-done = f32[2048,128]{1,0:T(8,128)} async-done(((f32[2048,128]{1,0:T(8,128)}), f32[2048,128]{1,0:T(8,128)}) %all-reduce.3.cloned.1.call-update) | async-done | bytes 1048592 | tf_op jit(solution)/shard_map/psum | solution.py:63
  398.3 2.4 fusion.12
  (88 shorter events, 35.7 us)
Async XLA Ops:
  7.2 63.2 %copy-start = (bf16[2048,128]{1,0:T(8,128)(2,1)S(1)}, bf16[2048,128]{1,0:T(8,128)(2,1)}, u32[]{:S(2)}) copy-start(bf16[2048,128]{1,0:T(8,128)(2,1)} %param.15) | copy-start | bytes 1572868
  7.2 46.0 %all-gather.2.cloned.1.call-start = ((), (), s32[]{:S(2)}) async-start(), calls=%async_computation | async-start | bytes 1572864 | tf_op jit(solution)/shard_map/all_gather | solution.py:18
  7.9 324.9 %all-reduce.5.cloned.1.call-start = ((), (), s32[]{:S(2)}) async-start(), calls=%async_computation.2 | async-start | bytes 524288 | tf_op jit(solution)/shard_map/psum | solution.py:74
  54.9 15.4 %copy-start.8 = (s32[1,8]{1,0:T(1,128)S(1)}, s32[1,8]{1,0:T(1,128)}, u32[]{:S(2)}) copy-start(s32[1,8]{1,0:T(1,128)} %param.23) | copy-start | bytes 100
  54.9 15.5 %copy-start.2 = (bf16[2048,256]{1,0:T(8,128)(2,1)S(1)}, bf16[2048,256]{1,0:T(8,128)(2,1)}, u32[]{:S(2)}) copy-start(bf16[2048,256]{1,0:T(8,128)(2,1)} %all-gather.2.cloned.1.call-done) | copy-start | bytes 3145732
  54.9 13.9 %collective-permute-start.1 = (bf16[16,128,128]{2,1,0:T(8,128)(2,1)S(1)}, bf16[16,128,128]{2,1,0:T(8,128)(2,1)S(1)}, u32[]{:S(2)}, u32[]{:S(2)}) collective-permute-start(bf16[16,128,128]{2,1,0:T(8,128)(2,1)S(1)} %bitcast.55), channel_id=1, source_target_pairs={{192,0},{200,8},{208,16},{216,24},{224,32},{232,40},{240,48},{248,... | collective-permute-start | bytes 1572872 | tf_op jit(solution)/shard_map/ppermute | solution.py:12
  56.7 14.0 %copy-start.6 = (bf16[2048,128]{1,0:T(8,128)(2,1)S(1)}, bf16[2048,128]{1,0:T(8,128)(2,1)}, u32[]{:S(2)}) copy-start(bf16[2048,128]{1,0:T(8,128)(2,1)} %param.14) | copy-start | bytes 1572868
  68.8 23.1 %collective-permute-start.2 = (bf16[16,128,128]{2,1,0:T(8,128)(2,1)S(1)}, bf16[16,128,128]{2,1,0:T(8,128)(2,1)S(1)}, u32[]{:S(2)}, u32[]{:S(2)}) collective-permute-start(bf16[16,128,128]{2,1,0:T(8,128)(2,1)S(1)} %broadcast_select_fusion), channel_id=1, source_target_pairs={{128,0},{136,8},{144,16},{152,24},{160,32},{168,40},{176,48},{184,... | collective-permute-start | bytes 1572872 | tf_op jit(solution)/shard_map/ppermute | solution.py:12
  71.8 326.5 %all-reduce.3.cloned.1.call-start = ((), (), s32[]{:S(2)}) async-start(), calls=%async_computation.1 | async-start | bytes 2097152 | tf_op jit(solution)/shard_map/psum | solution.py:63
  91.9 1.9 copy-start.4
  98.5 6.6 %copy-start.5 = (bf16[16,128,128]{2,1,0:T(8,128)(2,1)S(1)}, bf16[16,128,128]{2,1,0:T(8,128)(2,1)}, u32[]{:S(2)}) copy-start(bf16[16,128,128]{2,1,0:T(8,128)(2,1)} %copy-done.4) | copy-start | bytes 1572868
  105.1 12.4 %collective-permute-start = (bf16[16,128,128]{2,1,0:T(8,128)(2,1)S(1)}, bf16[16,128,128]{2,1,0:T(8,128)(2,1)S(1)}, u32[]{:S(2)}, u32[]{:S(2)}) collective-permute-start(bf16[16,128,128]{2,1,0:T(8,128)(2,1)S(1)} %get-tuple-element.305), channel_id=1, source_target_pairs={{248,0},{0,8},{8,16},{16,24},{24,32},{32,40},{40,48},{48,56},{56,6... | collective-permute-start | bytes 1572872 | tf_op jit(solution)/shard_map/while/body/eval_jaxpr/ppermute | solution.py:12
  128.5 10.9 %collective-permute-start = (bf16[16,128,128]{2,1,0:T(8,128)(2,1)S(1)}, bf16[16,128,128]{2,1,0:T(8,128)(2,1)S(1)}, u32[]{:S(2)}, u32[]{:S(2)}) collective-permute-start(bf16[16,128,128]{2,1,0:T(8,128)(2,1)S(1)} %get-tuple-element.305), channel_id=1, source_target_pairs={{248,0},{0,8},{8,16},{16,24},{24,32},{32,40},{40,48},{48,56},{56,6... | collective-permute-start | bytes 1572872 | tf_op jit(solution)/shard_map/while/body/eval_jaxpr/ppermute | solution.py:12
  150.4 10.9 %collective-permute-start = (bf16[16,128,128]{2,1,0:T(8,128)(2,1)S(1)}, bf16[16,128,128]{2,1,0:T(8,128)(2,1)S(1)}, u32[]{:S(2)}, u32[]{:S(2)}) collective-permute-start(bf16[16,128,128]{2,1,0:T(8,128)(2,1)S(1)} %get-tuple-element.305), channel_id=1, source_target_pairs={{248,0},{0,8},{8,16},{16,24},{24,32},{32,40},{40,48},{48,56},{56,6... | collective-permute-start | bytes 1572872 | tf_op jit(solution)/shard_map/while/body/eval_jaxpr/ppermute | solution.py:12
  172.2 10.9 %collective-permute-start = (bf16[16,128,128]{2,1,0:T(8,128)(2,1)S(1)}, bf16[16,128,128]{2,1,0:T(8,128)(2,1)S(1)}, u32[]{:S(2)}, u32[]{:S(2)}) collective-permute-start(bf16[16,128,128]{2,1,0:T(8,128)(2,1)S(1)} %get-tuple-element.305), channel_id=1, source_target_pairs={{248,0},{0,8},{8,16},{16,24},{24,32},{32,40},{40,48},{48,56},{56,6... | collective-permute-start | bytes 1572872 | tf_op jit(solution)/shard_map/while/body/eval_jaxpr/ppermute | solution.py:12
  194.1 10.8 %collective-permute-start = (bf16[16,128,128]{2,1,0:T(8,128)(2,1)S(1)}, bf16[16,128,128]{2,1,0:T(8,128)(2,1)S(1)}, u32[]{:S(2)}, u32[]{:S(2)}) collective-permute-start(bf16[16,128,128]{2,1,0:T(8,128)(2,1)S(1)} %get-tuple-element.305), channel_id=1, source_target_pairs={{248,0},{0,8},{8,16},{16,24},{24,32},{32,40},{40,48},{48,56},{56,6... | collective-permute-start | bytes 1572872 | tf_op jit(solution)/shard_map/while/body/eval_jaxpr/ppermute | solution.py:12
  215.9 10.8 %collective-permute-start = (bf16[16,128,128]{2,1,0:T(8,128)(2,1)S(1)}, bf16[16,128,128]{2,1,0:T(8,128)(2,1)S(1)}, u32[]{:S(2)}, u32[]{:S(2)}) collective-permute-start(bf16[16,128,128]{2,1,0:T(8,128)(2,1)S(1)} %get-tuple-element.305), channel_id=1, source_target_pairs={{248,0},{0,8},{8,16},{16,24},{24,32},{32,40},{40,48},{48,56},{56,6... | collective-permute-start | bytes 1572872 | tf_op jit(solution)/shard_map/while/body/eval_jaxpr/ppermute | solution.py:12
  237.6 10.9 %collective-permute-start = (bf16[16,128,128]{2,1,0:T(8,128)(2,1)S(1)}, bf16[16,128,128]{2,1,0:T(8,128)(2,1)S(1)}, u32[]{:S(2)}, u32[]{:S(2)}) collective-permute-start(bf16[16,128,128]{2,1,0:T(8,128)(2,1)S(1)} %get-tuple-element.305), channel_id=1, source_target_pairs={{248,0},{0,8},{8,16},{16,24},{24,32},{32,40},{40,48},{48,56},{56,6... | collective-permute-start | bytes 1572872 | tf_op jit(solution)/shard_map/while/body/eval_jaxpr/ppermute | solution.py:12
  259.5 1.0 copy-start.1
  259.5 138.8 %copy-start.3 = (bf16[2048,256]{1,0:T(8,128)(2,1)S(1)}, bf16[2048,256]{1,0:T(8,128)(2,1)}, u32[]{:S(2)}) copy-start(bf16[2048,256]{1,0:T(8,128)(2,1)} %all-gather.2.cloned.1.call-done) | copy-start | bytes 3145732
  259.5 138.8 %copy-start.7 = (bf16[128,256]{1,0:T(8,128)(2,1)S(1)}, bf16[128,256]{1,0:T(8,128)(2,1)}, u32[]{:S(2)}) copy-start(bf16[128,256]{1,0:T(8,128)(2,1)} %param.17) | copy-start | bytes 196612
Sparse Core Ops, SparseCore 0:
  9.8 43.3 all-gather.1
  71.9 260.8 all-reduce.4
  335.3 62.8 all-reduce.2
where the time goes:
time: 410 us; the launch traced here: 407 us
  waiting for transfers between devices  272 us (66%)
  other arithmetic  71.3 us (17%)
  matrix products  32.2 us (8%)
  local copies, waits for them, and re-layouts  15.1 us (4%)
  between operations  13.9 us (3%)
    ppermute x9, waiting for transfers between devices, passed_along(): return lax.ppermute(block, axis, route)  90.5 us
    psum x1, waiting for transfers between devices, shards(): summed = lax.psum(partial_sums, 'blk')  72.4 us
    psum x1, waiting for transfers between devices, shards(): neighbour = lax.psum(accumulated.reshape(row_count, feature_width), 'rep')  63.8 us
    scatter-add x8, other arithmetic, contribute(): return accumulated.at[targets].add(product)  52.4 us
    all_gather x1, waiting for transfers between devices, shards(): cotangent = lax.all_gather(grad_out, 'col', axis=1, tiled=True)  44.5 us
    dot_general x8, matrix products, contribute(): jnp.einsum('tab,taf->tbf', edge_values, picked, preferred_element_type=jn...  27.4 us
    and x8, other arithmetic, contribute(): picked = jnp.take(current, sources, axis=0)  10.1 us
  transfers between devices with their start and end apart: 12, of which 12 were waited for; matrix products, arithmetic and copies ran while one was open for 28% of the time, Pallas kernels for 0%

commit v1 on v0

v1 whole, which is shorter than its diff:
```python
import functools
import math

import jax
import jax.numpy as jnp
from jax import lax
from jax.experimental import pallas as pl
from jax.experimental.pallas import tpu as pltpu
from jax.sharding import PartitionSpec as P

NZ, NY, NC, NR = 4, 4, 2, 4
BLK = NZ * NY * NC
TILE = 128
NT = 16
HALF = 64
BF = jnp.bfloat16
F32 = jnp.float32
VMEM = pl.BlockSpec(memory_space=pltpu.VMEM)
SMEM = pl.BlockSpec(memory_space=pltpu.SMEM)
ANY = pl.BlockSpec(memory_space=pl.ANY)


def place(z, y, core):
    return ((z % NZ) * NY + y % NY) * NC + core


def send(x, move):
    route = []
    for b in range(BLK):
        z, y, core = b // (NY * NC), b // NC % NY, b % NC
        for r in range(NR):
            z2, y2, core2, r2 = move(z, y, core, r)
            route.append((b * NR + r, place(z2, y2, core2) * NR + r2 % NR))
    return lax.ppermute(x, ("blk", "rep"), route)


def to_core(z, y, core, r):
    return z, y, 1 - core, r


def to_row(z, y, core, r):
    if core == 0:
        dz, to = ((1, 1), (0, 0), (2, 2), (-1, 3))[r]
    else:
        dz, to = ((1, 0), (2, 1), (0, 3), (-1, 2))[r]
    return z + dz, y, core, to


def along(steps):
    def move(z, y, core, r):
        if core == 0:
            return z, y + steps, core, r if y + steps < NY else r - 1
        return z, y - steps, core, r if y >= steps else r + 1

    return move


def send_y(x, s):
    return send(x, lambda z, y, core, r: (z, y + s, core, r))


def send_z(x, s):
    return send(x, lambda z, y, core, r: (z + s, y, core, r))


def send_rep(x, s):
    return lax.ppermute(x, "rep", [(r, (r + s) % NR) for r in range(NR)])


def send_col(x):
    return lax.ppermute(x, "col", [(0, 1), (1, 0)])


def sds(shape, dtype):
    return jax.ShapeDtypeStruct(shape, dtype)


def params(mib=40):
    return pltpu.CompilerParams(vmem_limit_bytes=mib << 20)


def cost(flops, nbytes):
    return pl.CostEstimate(flops=flops, bytes_accessed=nbytes, transcendentals=0)


def prep_kernel(ids, g, deg, keep, give):
    flip = ids[0] == 1
    for t in range(NT):
        scale = 1.0 / deg[pl.ds(t, 1), :].astype(F32)
        turned = (jnp.transpose(g[t].astype(F32)) * scale).astype(BF)
        low, high = turned[:HALF], turned[HALF:]
        keep[t] = jnp.where(flip, high, low)
        give[t] = jnp.where(flip, low, high)


def prep(ids, g, deg):
    half = sds((NT, HALF, TILE), BF)
    return pl.pallas_call(
        prep_kernel,
        out_shape=(half, half),
        in_specs=[SMEM, VMEM, VMEM],
        out_specs=(VMEM, VMEM),
        compiler_params=params(8),
        cost_estimate=cost(1 << 20, 1 << 20),
        name="prep",
    )(ids, g, deg)


GROUP = 4


def spmm_kernel(items, last, plan, rows, cols, counts, tv, *refs):
    n = len(items)
    arrays = 2 * (1 + max(k for k, _ in items))
    sources, refs = refs[:arrays], refs[arrays:]
    if last:
        before, own, *outs, acc = refs
        acc[pl.ds(0, NT)] = before[...]
    else:
        after, acc = refs
        acc[...] = jnp.zeros_like(acc)
    slots = tv.shape[1]
    for i, (k, parity) in enumerate(items):
        mine, theirs = sources[2 * k], sources[2 * k + 1]
        j = jnp.maximum(plan[i], 0)
        live = jnp.where(plan[i] >= 0, jnp.clip(counts[0, j], 0, slots), 0)

        @pl.loop(0, (live + (GROUP - 1)) >> 2)
        def _(g, j=j, live=live, mine=mine, theirs=theirs, parity=parity):
            products, targets = [], []
            for u in range(GROUP):
                t = g * GROUP + u
                row = rows[j, t]
                source = jnp.concatenate([mine[parity, row], theirs[1 - parity, row]], axis=0)
                products.append(jnp.dot(source, tv[j, t], preferred_element_type=F32))
                targets.append(jnp.where(t < live, cols[j, t], NT))
            for target, product in zip(targets, products):
                acc[target] += product

    if last:
        me = plan[n]
        q = NT // NR
        for i in range(q):
            own[i] = acc[me * q + i]
            for s in range(1, NR):
                to = (me + s) % NR
                outs[s - 1][i] = acc[to * q + i].astype(BF)
    else:
        after[...] = acc[pl.ds(0, NT)]


def spmm(plan, tables, tv, items, pairs, before=None):
    last = before is not None
    flat = [x for pair in pairs for x in pair]
    q = NT // NR
    if last:
        out_shape = (sds((q, TILE, TILE), F32),) + (sds((q, TILE, TILE), BF),) * 3
        out_specs = (VMEM,) * 4
    else:
        out_shape, out_specs = sds((NT, TILE, TILE), F32), VMEM
    return pl.pallas_call(
        functools.partial(spmm_kernel, items, last),
        out_shape=out_shape,
        in_specs=[SMEM] * 4 + [VMEM] * (1 + len(flat) + last),
        out_specs=out_specs,
        scratch_shapes=[pltpu.VMEM((NT + 1, TILE, TILE), F32)],
        compiler_params=params(20),
        cost_estimate=cost(len(items) * 10 * 2 * TILE**3, len(items) << 20),
        name="tiles",
    )(plan, *tables, tv, *flat, *([before] if last else []))


def finish_kernel(mine, theirs, wn, self_term, out):
    for t in range(NT // NR):
        y = jnp.concatenate([mine[t], theirs[t]], axis=0)
        turned = jnp.dot(wn[...], y, preferred_element_type=F32)
        rows = pl.ds(t * TILE, TILE)
        out[rows, :] = (self_term[rows, :] + jnp.transpose(turned)).astype(BF)


def finish(mine, theirs, wn, self_term):
    return pl.pallas_call(
        finish_kernel,
        out_shape=sds(self_term.shape, BF),
        in_specs=[VMEM] * 4,
        out_specs=VMEM,
        compiler_params=params(8),
        cost_estimate=cost(2 * 512 * 256 * 128, 1 << 19),
        name="finish",
    )(mine, theirs, wn, self_term)


def in_order(parts, me, axis):
    n = len(parts)
    slots = jnp.stack(parts[::-1] * 2)
    at = (n - 1 - me) % n
    return jnp.concatenate(
        [
            lax.dynamic_index_in_dim(slots, at + i, 0, keepdims=False)
            for i in range(n)
        ],
        axis=axis,
    )


def reduce_pieces(x, me, move, n):
    total = lax.dynamic_index_in_dim(x, me, 0, keepdims=False)
    for s in range(1, n):
        total = total + move(
            lax.dynamic_index_in_dim(x, (me + s) % n, 0, keepdims=False), s
        )
    return total


def weight_sum(partial, y, rep):
    by_rep = partial.reshape(2, NR, -1, 256).transpose(1, 0, 2, 3)
    mine = reduce_pieces(by_rep, rep, send_rep, NR)
    by_y = mine.reshape(2, NY, -1, 256).transpose(1, 0, 2, 3)
    mine = reduce_pieces(by_y, y, send_y, NY)
    mine = mine + sum(send_z(mine, s) for s in range(1, NZ))
    mine = mine + send(mine, to_core)
    mine = in_order([mine] + [send_y(mine, s) for s in range(1, NY)], y, 1)
    return in_order([mine] + [send_rep(mine, s) for s in range(1, NR)], rep, 1)


def shards(
    feats, agg_feats, grad_out, w_self, w_neigh, degree, tile_vals, tile_rows, tile_cols, tile_count
):
    blk, rep, col = (lax.axis_index(a) for a in ("blk", "rep", "col"))
    core, y = blk % NC, blk // NC % NY
    ids = jnp.stack([core, y, rep]).astype(jnp.int32)
    row_count, width = feats.shape
    quarter = row_count // NR
    tables = (tile_rows[0], tile_cols[0], tile_count)
    tv = tile_vals[0]

    keep, give = prep(ids, grad_out.reshape(NT, TILE, width), degree.reshape(NT, TILE))
    held = jnp.stack([keep, send(give, to_core)])
    near = send(held, to_row)
    step1 = send(near, along(1))
    step3 = send(near, along(3))
    far = send(near, lambda z, y, core, r: (z, y, core, r - 1 if core == 0 else r + 1))
    step2 = send(step1, along(1))
    near_x, step1_x, step3_x, far_x, step2_x = (
        send(x, to_core) for x in (near, step1, step3, far, step2)
    )
    pairs = [(near, far_x), (step1, step3_x), (step3, step1_x), (far, near_x)]
    outer = [((0, 0), 0, -1), ((3, 0), -1, 0), ((3, 1), 7, 1)]
    outer += [((1, 0), 2, 6), ((1, 1), 1, 7), ((2, 0), 6, 2), ((2, 1), 5, 3)]
    inner = [((0, 0), 4, 4), ((0, 1), 3, 5)]
    plan = lambda table: [jnp.where(core == 0, a, b) for _, a, b in table]
    acc = spmm(jnp.stack(plan(outer)), tables, tv, [i for i, _, _ in outer], pairs)
    own, *outs = spmm(
        jnp.stack(plan(inner) + [rep]), tables, tv, [i for i, _, _ in inner], [(step2, step2_x)], acc
    )
    total = own
    for shift, piece in enumerate(outs, 1):
        total = total + send_rep(piece, shift).astype(F32)
    mine = total.astype(BF)

    rows = lambda x: lax.dynamic_slice_in_dim(x, rep * quarter, quarter, 0)
    g_own = rows(grad_out)
    g_other = send_col(g_own)
    g_rows = jnp.where(
        col == 0,
        jnp.concatenate([g_own, g_other], axis=1),
        jnp.concatenate([g_other, g_own], axis=1),
    )
    self_term = lax.dot_general(
        g_rows, w_self, (((1,), (1,)), ((), ())), preferred_element_type=F32
    )
    over_rows = (((0,), (0,)), ((), ()))
    partial = jnp.stack(
        [
            lax.dot_general(rows(x), g_rows, over_rows, preferred_element_type=F32)
            for x in (feats, agg_feats)
        ]
    )
    node_count = row_count * lax.axis_size("blk")
    grad_weight = weight_sum(partial, y, rep) * (1.0 / math.sqrt(node_count))

    own_first = [jnp.where(col == 0, w_neigh[:, i : i + HALF], w_neigh[:, width + i : width + i + HALF]) for i in (0, HALF)]
    other = [jnp.where(col == 0, w_neigh[:, width + i : width + i + HALF], w_neigh[:, i : i + HALF]) for i in (0, HALF)]
    turn = lambda pair: [jnp.where(core == 0, *pair), jnp.where(core == 0, *pair[::-1])]
    wn = jnp.concatenate(turn(own_first) + turn(other), axis=1)
    block = finish(mine, send_col(mine), wn, self_term)
    grad_feats = in_order([block] + [send_rep(block, s) for s in range(1, NR)], rep, 0)
    return (grad_feats, grad_weight)


def solution(mesh):
    placed = (
        P("blk", "col"),
        P("blk", "col"),
        P("blk", "col"),
        P("col", None),
        P("col", None),
        P("blk"),
        P("blk", "rep", None, None, None),
        P("blk", "rep", None),
        P("blk", "rep", None),
        P("blk", "rep"),
    )
    return jax.shard_map(
        shards,
        mesh=mesh,
        in_specs=placed,
        out_specs=(P("blk", "col"), P(None, "col", None)),
        check_vma=False,
    )
```

time: 410 us -> 143 us (0.35)
  waiting for transfers between devices: 272 us -> 47.8 us
  other arithmetic: 71.3 us -> 2.93 us
  starting transfers between devices: 2.59 us -> 67.5 us
  matrix products: 32.2 us -> 2.43 us
  between operations: 13.9 us -> 1.09 us
  Pallas kernels: 0 us -> 8.05 us
    psum x2 -> x0, waiting for transfers between devices: 136 us -> none  [the longest x1 72.4 us: shards(): summed = lax.psum(partial_sums, 'blk')]
    ppermute x9 -> x35, starting transfers between devices: 2.48 us -> 67.5 us  [the longest x21 29.3 us: send(): return lax.ppermute(x, ('blk', 'rep'), route)]
    scatter-add x8 -> x0, other arithmetic: 52.4 us -> none  [contribute(): return accumulated.at[targets].add(product)]
    all_gather x1 -> x0, waiting for transfers between devices: 44.5 us -> none  [shards(): cotangent = lax.all_gather(grad_out, 'col', axis=1, tiled=True)]
    ppermute x9 -> x35, waiting for transfers between devices: 90.5 us -> 47.8 us  [the longest x21 22.3 us: send(): return lax.ppermute(x, ('blk', 'rep'), route)]
    dot_general x12 -> x3, matrix products: 32.2 us -> 2.43 us  [the longest x2 1.37 us: shards(): lax.dot_general(rows(x), g_rows, over_rows, preferred_element_type=F32)]
    unnamed x18 -> x42, local copies, waits for them, and re-layouts: 1.02 us -> 11.9 us
    and x8 -> x0, other arithmetic: 10.1 us -> none  [contribute(): picked = jnp.take(current, sources, axis=0)]
  transfers between devices with their start and end apart: 12 -> 35, of which waited for: 12 -> 16; matrix products, arithmetic and copies ran while one was open for 28% -> 2% of each run, Pallas kernels for 0% -> 4%
where the time goes in v1:
time: 143 us
  starting transfers between devices  67.5 us (47%)
  waiting for transfers between devices  47.8 us (33%)
  local copies, waits for them, and re-layouts  13.1 us (9%)
  Pallas kernels  8.05 us (6%)
  other arithmetic  2.93 us (2%)
  matrix products  2.43 us (2%)
    ppermute x21, starting transfers between devices, send(): return lax.ppermute(x, ('blk', 'rep'), route)  29.3 us
    ppermute x12, starting transfers between devices, send_rep(): return lax.ppermute(x, 'rep', [(r, (r + s) % NR) for r in range(NR)])  25.8 us
    ppermute x21, waiting for transfers between devices, send(): return lax.ppermute(x, ('blk', 'rep'), route)  22.3 us
    ppermute x2, waiting for transfers between devices, send_col(): return lax.ppermute(x, 'col', [(0, 1), (1, 0)])  13 us
    ppermute x12, waiting for transfers between devices, send_rep(): return lax.ppermute(x, 'rep', [(r, (r + s) % NR) for r in range(NR)])  12.5 us
    ppermute x2, starting transfers between devices, send_col(): return lax.ppermute(x, 'col', [(0, 1), (1, 0)])  12.4 us
    unnamed x42, local copies, waits for them, and re-layouts  11.9 us
    pallas_call x2, Pallas kernels, spmm(): pl.pallas_call(functools.partial(spmm_kernel, items, last), out_shape=out...  6.99 us
  transfers between devices with their start and end apart: 35, of which 16 were waited for; matrix products, arithmetic and copies ran while one was open for 2% of the time, Pallas kernels for 4%

profile of v1, /device:TPU:32, one launch (start us, length us, event | category | flops | bytes accessed | tf_op | source)
XLA Modules:
  0.0 142.9 jit_solution(7102279933113277477)
XLA Ops:
  1.6 6.4 %collective-permute-start.15 = (bf16[512,128]{1,0:T(8,128)(2,1)S(1)}, bf16[512,128]{1,0:T(8,128)(2,1)S(1)}, u32[]{:S(2)}, u32[]{:S(2)}) collective-permute-start(bf16[512,128]{1,0:T(8,128)(2,1)S(1)} %constant_dynamic-slice_fusion), channel_id=1, source_target_pairs={{0,4},{4,0},{1,5},{5,1},{2,6},{6,2},{3,7},{7,3},{8,12},{12,8},{9,1... | collective-permute-start | bytes 393224 | tf_op jit(solution)/shard_map/ppermute | solution.py:71
  8.0 6.4 %collective-permute-done.15 = bf16[512,128]{1,0:T(8,128)(2,1)S(1)} collective-permute-done((bf16[512,128]{1,0:T(8,128)(2,1)S(1)}, bf16[512,128]{1,0:T(8,128)(2,1)S(1)}, u32[]{:S(2)}, u32[]{:S(2)}) %collective-permute-start.15) | collective-permute-done | bytes 131104 | tf_op jit(solution)/shard_map/ppermute | solution.py:71
  15.8 1.6 %collective-permute-start.19 = (f32[2,32,256]{2,1,0:T(8,128)S(1)}, f32[2,32,256]{2,1,0:T(8,128)S(1)}, u32[]{:S(2)}, u32[]{:S(2)}) collective-permute-start(f32[2,32,256]{2,1,0:T(8,128)S(1)} %get-tuple-element.22), channel_id=1, source_target_pairs={{0,1},{1,2},{2,3},{3,0},{4,5},{5,6},{6,7},{7,4},{8,9},{9,10},{10,1... | collective-permute-start | bytes 196616 | tf_op jit(solution)/shard_map/ppermute | solution.py:67
  17.3 2.7 %collective-permute-start.20 = (f32[2,32,256]{2,1,0:T(8,128)S(1)}, f32[2,32,256]{2,1,0:T(8,128)S(1)}, u32[]{:S(2)}, u32[]{:S(2)}) collective-permute-start(f32[2,32,256]{2,1,0:T(8,128)S(1)} %get-tuple-element.23), channel_id=1, source_target_pairs={{0,2},{1,3},{2,0},{3,1},{4,6},{5,7},{6,4},{7,5},{8,10},{9,11},{10,... | collective-permute-start | bytes 196616 | tf_op jit(solution)/shard_map/ppermute | solution.py:67
  24.4 1.7 %collective-permute-start.22 = (f32[2,8,256]{2,1,0:T(8,128)S(1)}, f32[2,8,256]{2,1,0:T(8,128)S(1)}, u32[]{:S(2)}, u32[]{:S(2)}) collective-permute-start(f32[2,8,256]{2,1,0:T(8,128)S(1)} %get-tuple-element.29), channel_id=1, source_target_pairs={{0,16},{1,17},{2,18},{3,19},{8,24},{9,25},{10,26},{11,27},{16,32},... | collective-permute-start | bytes 49160 | tf_op jit(solution)/shard_map/ppermute | solution.py:34
  26.1 2.9 %collective-permute-start.23 = (f32[2,8,256]{2,1,0:T(8,128)S(1)}, f32[2,8,256]{2,1,0:T(8,128)S(1)}, u32[]{:S(2)}, u32[]{:S(2)}) collective-permute-start(f32[2,8,256]{2,1,0:T(8,128)S(1)} %get-tuple-element.31), channel_id=1, source_target_pairs={{0,32},{1,33},{2,34},{3,35},{8,40},{9,41},{10,42},{11,43},{16,48},... | collective-permute-start | bytes 49160 | tf_op jit(solution)/shard_map/ppermute | solution.py:34
  32.7 1.5 %collective-permute-start.25 = (f32[2,8,256]{2,1,0:T(8,128)S(1)}, f32[2,8,256]{2,1,0:T(8,128)S(1)}, u32[]{:S(2)}, u32[]{:S(2)}) collective-permute-start(f32[2,8,256]{2,1,0:T(8,128)S(1)} %fusion.17), channel_id=1, source_target_pairs={{0,64},{1,65},{2,66},{3,67},{8,72},{9,73},{10,74},{11,75},{16,80},... | collective-permute-start | bytes 49160 | tf_op jit(solution)/shard_map/ppermute | solution.py:34
  34.2 1.6 %collective-permute-start.27 = (f32[2,8,256]{2,1,0:T(8,128)S(1)}, f32[2,8,256]{2,1,0:T(8,128)S(1)}, u32[]{:S(2)}, u32[]{:S(2)}) collective-permute-start(f32[2,8,256]{2,1,0:T(8,128)S(1)} %fusion.17), channel_id=1, source_target_pairs={{0,192},{1,193},{2,194},{3,195},{8,200},{9,201},{10,202},{11,203},... | collective-permute-start | bytes 49160 | tf_op jit(solution)/shard_map/ppermute | solution.py:34
  36.5 2.3 %collective-permute-done.26 = f32[2,8,256]{2,1,0:T(8,128)S(1)} collective-permute-done((f32[2,8,256]{2,1,0:T(8,128)S(1)}, f32[2,8,256]{2,1,0:T(8,128)S(1)}, u32[]{:S(2)}, u32[]{:S(2)}) %collective-permute-start.26) | collective-permute-done | bytes 16416 | tf_op jit(solution)/shard_map/ppermute | solution.py:34
  40.1 2.6 %collective-permute-start.29 = (f32[2,8,256]{2,1,0:T(8,128)S(1)}, f32[2,8,256]{2,1,0:T(8,128)S(1)}, u32[]{:S(2)}, u32[]{:S(2)}) collective-permute-start(f32[2,8,256]{2,1,0:T(8,128)S(1)} %add.228), channel_id=1, source_target_pairs={{0,48},{1,49},{2,50},{3,51},{8,56},{9,57},{10,58},{11,59},{16,0},{... | collective-permute-start | bytes 49160 | tf_op jit(solution)/shard_map/ppermute | solution.py:34
  44.8 3.0 %collective-permute-done.30 = f32[2,8,256]{2,1,0:T(8,128)S(1)} collective-permute-done((f32[2,8,256]{2,1,0:T(8,128)S(1)}, f32[2,8,256]{2,1,0:T(8,128)S(1)}, u32[]{:S(2)}, u32[]{:S(2)}) %collective-permute-start.30) | collective-permute-done | bytes 16416 | tf_op jit(solution)/shard_map/ppermute | solution.py:34
  47.9 7.8 %collective-permute-done.1.refs_0_ = bf16[2,16,64,128]{3,2,1,0:T(8,128)(2,1)S(1)} collective-permute-done((bf16[2,16,64,128]{3,2,1,0:T(8,128)(2,1)S(1)}, bf16[2,16,64,128]{3,2,1,0:T(8,128)(2,1)S(1)}, u32[]{:S(2)}, u32[]{:S(2)}) %collective-permute-start.1) | collective-permute-done | bytes 524320 | tf_op jit(solution)/shard_map/ppermute | solution.py:34
  55.8 2.3 %collective-permute-start.2 = (bf16[2,16,64,128]{3,2,1,0:T(8,128)(2,1)S(1)}, bf16[2,16,64,128]{3,2,1,0:T(8,128)(2,1)S(1)}, u32[]{:S(2)}, u32[]{:S(2)}) collective-permute-start(bf16[2,16,64,128]{3,2,1,0:T(8,128)(2,1)S(1)} %collective-permute-done.1.refs_0_), channel_id=1, source_target_pairs={{0,16},{1,17},{2,18},{3,19},{8,57},{9,58},{10,59},{11,56},{16,32},... | collective-permute-start | bytes 1572872 | tf_op jit(solution)/shard_map/ppermute | solution.py:34
  58.1 3.4 %collective-permute-start.32 = (f32[2,32,256]{2,1,0:T(8,128)S(1)}, f32[2,32,256]{2,1,0:T(8,128)S(1)}, u32[]{:S(2)}, u32[]{:S(2)}) collective-permute-start(f32[2,32,256]{2,1,0:T(8,128)S(1)} %pad_maximum_fusion.3), channel_id=1, source_target_pairs={{0,3},{1,0},{2,1},{3,2},{4,7},{5,4},{6,5},{7,6},{8,11},{9,8},{10,9... | collective-permute-start | bytes 196616 | tf_op jit(solution)/shard_map/ppermute | solution.py:67
  64.0 3.6 %collective-permute-done.2.refs_2_ = bf16[2,16,64,128]{3,2,1,0:T(8,128)(2,1)S(1)} collective-permute-done((bf16[2,16,64,128]{3,2,1,0:T(8,128)(2,1)S(1)}, bf16[2,16,64,128]{3,2,1,0:T(8,128)(2,1)S(1)}, u32[]{:S(2)}, u32[]{:S(2)}) %collective-permute-start.2) | collective-permute-done | bytes 524320 | tf_op jit(solution)/shard_map/ppermute | solution.py:34
  68.7 3.8 %collective-permute-start.33 = (f32[2,32,256]{2,1,0:T(8,128)S(1)}, f32[2,32,256]{2,1,0:T(8,128)S(1)}, u32[]{:S(2)}, u32[]{:S(2)}) collective-permute-start(f32[2,32,256]{2,1,0:T(8,128)S(1)} %pad_maximum_fusion.3), channel_id=1, source_target_pairs={{0,2},{1,3},{2,0},{3,1},{4,6},{5,7},{6,4},{7,5},{8,10},{9,11},{10,... | collective-permute-start | bytes 196616 | tf_op jit(solution)/shard_map/ppermute | solution.py:67
  72.5 3.5 %collective-permute-start.34 = (f32[2,32,256]{2,1,0:T(8,128)S(1)}, f32[2,32,256]{2,1,0:T(8,128)S(1)}, u32[]{:S(2)}, u32[]{:S(2)}) collective-permute-start(f32[2,32,256]{2,1,0:T(8,128)S(1)} %pad_maximum_fusion.3), channel_id=1, source_target_pairs={{0,1},{1,2},{2,3},{3,0},{4,5},{5,6},{6,7},{7,4},{8,9},{9,10},{10,1... | collective-permute-start | bytes 196616 | tf_op jit(solution)/shard_map/ppermute | solution.py:67
  76.1 7.8 %collective-permute-start.10 = (bf16[2,16,64,128]{3,2,1,0:T(8,128)(2,1)S(1)}, bf16[2,16,64,128]{3,2,1,0:T(8,128)(2,1)S(1)}, u32[]{:S(2)}, u32[]{:S(2)}) collective-permute-start(bf16[2,16,64,128]{3,2,1,0:T(8,128)(2,1)S(1)} %collective-permute-done.1.refs_0_), channel_id=1, source_target_pairs={{0,8},{1,9},{2,10},{3,11},{8,0},{9,1},{10,2},{11,3},{16,24},{17,25... | collective-permute-start | bytes 1572872 | tf_op jit(solution)/shard_map/ppermute | solution.py:34
  83.9 2.3 %collective-permute-start.9 = (bf16[2,16,64,128]{3,2,1,0:T(8,128)(2,1)S(1)}, bf16[2,16,64,128]{3,2,1,0:T(8,128)(2,1)S(1)}, u32[]{:S(2)}, u32[]{:S(2)}) collective-permute-start(bf16[2,16,64,128]{3,2,1,0:T(8,128)(2,1)S(1)} %collective-permute-done.2.refs_2_), channel_id=1, source_target_pairs={{0,8},{1,9},{2,10},{3,11},{8,0},{9,1},{10,2},{11,3},{16,24},{17,25... | collective-permute-start | bytes 1572872 | tf_op jit(solution)/shard_map/ppermute | solution.py:34
  86.9 1.6 %collective-permute-done.6.refs_1_ = bf16[2,16,64,128]{3,2,1,0:T(8,128)(2,1)S(1)} collective-permute-done((bf16[2,16,64,128]{3,2,1,0:T(8,128)(2,1)S(1)}, bf16[2,16,64,128]{3,2,1,0:T(8,128)(2,1)S(1)}, u32[]{:S(2)}, u32[]{:S(2)}) %collective-permute-start.6) | collective-permute-done | bytes 524320 | tf_op jit(solution)/shard_map/ppermute | solution.py:34
  89.3 4.0 %copy-done.1 = bf16[1,8,40,128,128]{4,3,2,1,0:T(8,128)(2,1)S(1)} copy-done((bf16[1,8,40,128,128]{4,3,2,1,0:T(8,128)(2,1)S(1)}, bf16[1,8,40,128,128]{4,3,2,1,0:T(8,128)(2,1)}, u32[]{:S(2)}) %copy-start.1) | copy-done | bytes 10485784
  95.3 5.4 %tiles.2.refs_2_ = f32[16,128,128]{2,1,0:T(8,128)S(1)} custom-call(s32[7]{0:T(128)S(1)} %stack.135.plan, s32[8,40]{1,0:T(8,128)S(1)} %bitcast.115, s32[8,40]{1,0:T(8,128)S(1)} %bitcast.117, s32[1,8]{1,0:T(1,128)S(1)} %copy-done.9, bf16[8,40,128,128]{3,2,1,0:T(8,128)(2,1)S(1)} %bitcast.111, bf16[2,16,64,128]{3,2,1,0:T(8,128)(2,1)S(1)} %collective-permute-done.1.refs_0_, ...), custom_call_target="tpu_custom_call" | custom-call | flops 293601280 | bytes 7340032 | tf_op jit(solution)/shard_map/tiles/pallas_call | solution.py:161
  100.8 4.0 %copy-done.2 = bf16[1,8,40,128,128]{4,3,2,1,0:T(8,128)(2,1)S(1)} copy-done((bf16[1,8,40,128,128]{4,3,2,1,0:T(8,128)(2,1)S(1)}, bf16[1,8,40,128,128]{4,3,2,1,0:T(8,128)(2,1)}, u32[]{:S(2)}) %copy-start.2) | copy-done | bytes 10485784
  104.7 1.5 %tiles.3 = (f32[4,128,128]{2,1,0:T(8,128)S(1)}, bf16[4,128,128]{2,1,0:T(8,128)(2,1)S(1)}, bf16[4,128,128]{2,1,0:T(8,128)(2,1)S(1)}, bf16[4,128,128]{2,1,0:T(8,128)(2,1)S(1)}) custom-call(s32[3]{0:T(128)S(1)} %add_add_fusion.1.plan, s32[8,40]{1,0:T(8,128)S(1)} %bitcast.116, s32[8,40]{1,0:T(8,128)S(1)} %bitcast.118, s32[1,8]{1,0:T(1,128)S(1)} %copy-done.10, ...), custom_call_target="tpu_custom_call" | custom-call | flops 83886080 | bytes 2097152 | tf_op jit(solution)/shard_map/tiles/pallas_call | solution.py:161
  106.4 2.5 %collective-permute-start.12 = (bf16[4,128,128]{2,1,0:T(8,128)(2,1)S(1)}, bf16[4,128,128]{2,1,0:T(8,128)(2,1)S(1)}, u32[]{:S(2)}, u32[]{:S(2)}) collective-permute-start(bf16[4,128,128]{2,1,0:T(8,128)(2,1)S(1)} %get-tuple-element.12), channel_id=1, source_target_pairs={{0,2},{1,3},{2,0},{3,1},{4,6},{5,7},{6,4},{7,5},{8,10},{9,11},{10,... | collective-permute-start | bytes 393224 | tf_op jit(solution)/shard_map/ppermute | solution.py:67
  108.9 2.1 %collective-permute-start.13 = (bf16[4,128,128]{2,1,0:T(8,128)(2,1)S(1)}, bf16[4,128,128]{2,1,0:T(8,128)(2,1)S(1)}, u32[]{:S(2)}, u32[]{:S(2)}) collective-permute-start(bf16[4,128,128]{2,1,0:T(8,128)(2,1)S(1)} %get-tuple-element.13), channel_id=1, source_target_pairs={{0,3},{1,0},{2,1},{3,2},{4,7},{5,4},{6,5},{7,6},{8,11},{9,8},{10,9... | collective-permute-start | bytes 393224 | tf_op jit(solution)/shard_map/ppermute | solution.py:67
  111.1 4.6 %collective-permute-done.11 = bf16[4,128,128]{2,1,0:T(8,128)(2,1)S(1)} collective-permute-done((bf16[4,128,128]{2,1,0:T(8,128)(2,1)S(1)}, bf16[4,128,128]{2,1,0:T(8,128)(2,1)S(1)}, u32[]{:S(2)}, u32[]{:S(2)}) %collective-permute-start.11) | collective-permute-done | bytes 131104 | tf_op jit(solution)/shard_map/ppermute | solution.py:67
  116.7 6.0 %collective-permute-start.14 = (bf16[4,128,128]{2,1,0:T(8,128)(2,1)S(1)}, bf16[4,128,128]{2,1,0:T(8,128)(2,1)S(1)}, u32[]{:S(2)}, u32[]{:S(2)}) collective-permute-start(bf16[4,128,128]{2,1,0:T(8,128)(2,1)S(1)} %add_convert_fusion.mine), channel_id=1, source_target_pairs={{0,4},{4,0},{1,5},{5,1},{2,6},{6,2},{3,7},{7,3},{8,12},{12,8},{9,1... | collective-permute-start | bytes 393224 | tf_op jit(solution)/shard_map/ppermute | solution.py:71
  122.7 6.6 %collective-permute-done.14.theirs = bf16[4,128,128]{2,1,0:T(8,128)(2,1)S(1)} collective-permute-done((bf16[4,128,128]{2,1,0:T(8,128)(2,1)S(1)}, bf16[4,128,128]{2,1,0:T(8,128)(2,1)S(1)}, u32[]{:S(2)}, u32[]{:S(2)}) %collective-permute-start.14) | collective-permute-done | bytes 131104 | tf_op jit(solution)/shard_map/ppermute | solution.py:71
  129.6 3.7 %collective-permute-start.16 = (bf16[512,128]{1,0:T(8,128)(2,1)S(1)}, bf16[512,128]{1,0:T(8,128)(2,1)S(1)}, u32[]{:S(2)}, u32[]{:S(2)}) collective-permute-start(bf16[512,128]{1,0:T(8,128)(2,1)S(1)} %finish.1), channel_id=1, source_target_pairs={{0,3},{1,0},{2,1},{3,2},{4,7},{5,4},{6,5},{7,6},{8,11},{9,8},{10,9... | collective-permute-start | bytes 393224 | tf_op jit(solution)/shard_map/ppermute | solution.py:67
  134.9 3.1 %collective-permute-done.16 = bf16[512,128]{1,0:T(8,128)(2,1)S(1)} collective-permute-done((bf16[512,128]{1,0:T(8,128)(2,1)S(1)}, bf16[512,128]{1,0:T(8,128)(2,1)S(1)}, u32[]{:S(2)}, u32[]{:S(2)}) %collective-permute-start.16) | collective-permute-done | bytes 131104 | tf_op jit(solution)/shard_map/ppermute | solution.py:67
  137.9 2.6 %collective-permute-done.17 = bf16[512,128]{1,0:T(8,128)(2,1)S(1)} collective-permute-done((bf16[512,128]{1,0:T(8,128)(2,1)S(1)}, bf16[512,128]{1,0:T(8,128)(2,1)S(1)}, u32[]{:S(2)}, u32[]{:S(2)}) %collective-permute-start.17) | collective-permute-done | bytes 131104 | tf_op jit(solution)/shard_map/ppermute | solution.py:67
  (111 shorter events, 26.9 us)
Async XLA Ops:
  1.6 12.7 %collective-permute-start.15 = (bf16[512,128]{1,0:T(8,128)(2,1)S(1)}, bf16[512,128]{1,0:T(8,128)(2,1)S(1)}, u32[]{:S(2)}, u32[]{:S(2)}) collective-permute-start(bf16[512,128]{1,0:T(8,128)(2,1)S(1)} %constant_dynamic-slice_fusion), channel_id=1, source_target_pairs={{0,4},{4,0},{1,5},{5,1},{2,6},{6,2},{3,7},{7,3},{8,12},{12,8},{9,1... | collective-permute-start | bytes 393224 | tf_op jit(solution)/shard_map/ppermute | solution.py:71
  15.8 8.5 %collective-permute-start.19 = (f32[2,32,256]{2,1,0:T(8,128)S(1)}, f32[2,32,256]{2,1,0:T(8,128)S(1)}, u32[]{:S(2)}, u32[]{:S(2)}) collective-permute-start(f32[2,32,256]{2,1,0:T(8,128)S(1)} %get-tuple-element.22), channel_id=1, source_target_pairs={{0,1},{1,2},{2,3},{3,0},{4,5},{5,6},{6,7},{7,4},{8,9},{9,10},{10,1... | collective-permute-start | bytes 196616 | tf_op jit(solution)/shard_map/ppermute | solution.py:67
  17.3 6.9 %collective-permute-start.20 = (f32[2,32,256]{2,1,0:T(8,128)S(1)}, f32[2,32,256]{2,1,0:T(8,128)S(1)}, u32[]{:S(2)}, u32[]{:S(2)}) collective-permute-start(f32[2,32,256]{2,1,0:T(8,128)S(1)} %get-tuple-element.23), channel_id=1, source_target_pairs={{0,2},{1,3},{2,0},{3,1},{4,6},{5,7},{6,4},{7,5},{8,10},{9,11},{10,... | collective-permute-start | bytes 196616 | tf_op jit(solution)/shard_map/ppermute | solution.py:67
  20.1 4.3 %collective-permute-start.21 = (f32[2,32,256]{2,1,0:T(8,128)S(1)}, f32[2,32,256]{2,1,0:T(8,128)S(1)}, u32[]{:S(2)}, u32[]{:S(2)}) collective-permute-start(f32[2,32,256]{2,1,0:T(8,128)S(1)} %get-tuple-element.24), channel_id=1, source_target_pairs={{0,3},{1,0},{2,1},{3,2},{4,7},{5,4},{6,5},{7,6},{8,11},{9,8},{10,9... | collective-permute-start | bytes 196616 | tf_op jit(solution)/shard_map/ppermute | solution.py:67
  24.1 19.5 %collective-permute-start = (bf16[16,64,128]{2,1,0:T(8,128)(2,1)S(1)}, bf16[16,64,128]{2,1,0:T(8,128)(2,1)S(1)}, u32[]{:S(2)}, u32[]{:S(2)}) collective-permute-start(bf16[16,64,128]{2,1,0:T(8,128)(2,1)S(1)} %get-tuple-element.9), channel_id=1, source_target_pairs={{0,8},{1,9},{2,10},{3,11},{8,0},{9,1},{10,2},{11,3},{16,24},{17,25... | collective-permute-start | bytes 786440 | tf_op jit(solution)/shard_map/ppermute | solution.py:34
  24.4 6.9 %collective-permute-start.22 = (f32[2,8,256]{2,1,0:T(8,128)S(1)}, f32[2,8,256]{2,1,0:T(8,128)S(1)}, u32[]{:S(2)}, u32[]{:S(2)}) collective-permute-start(f32[2,8,256]{2,1,0:T(8,128)S(1)} %get-tuple-element.29), channel_id=1, source_target_pairs={{0,16},{1,17},{2,18},{3,19},{8,24},{9,25},{10,26},{11,27},{16,32},... | collective-permute-start | bytes 49160 | tf_op jit(solution)/shard_map/ppermute | solution.py:34
  26.1 5.2 %collective-permute-start.23 = (f32[2,8,256]{2,1,0:T(8,128)S(1)}, f32[2,8,256]{2,1,0:T(8,128)S(1)}, u32[]{:S(2)}, u32[]{:S(2)}) collective-permute-start(f32[2,8,256]{2,1,0:T(8,128)S(1)} %get-tuple-element.31), channel_id=1, source_target_pairs={{0,32},{1,33},{2,34},{3,35},{8,40},{9,41},{10,42},{11,43},{16,48},... | collective-permute-start | bytes 49160 | tf_op jit(solution)/shard_map/ppermute | solution.py:34
  29.0 3.7 %collective-permute-start.24 = (f32[2,8,256]{2,1,0:T(8,128)S(1)}, f32[2,8,256]{2,1,0:T(8,128)S(1)}, u32[]{:S(2)}, u32[]{:S(2)}) collective-permute-start(f32[2,8,256]{2,1,0:T(8,128)S(1)} %get-tuple-element.30), channel_id=1, source_target_pairs={{0,48},{1,49},{2,50},{3,51},{8,56},{9,57},{10,58},{11,59},{16,0},{... | collective-permute-start | bytes 49160 | tf_op jit(solution)/shard_map/ppermute | solution.py:34
  32.7 3.8 %collective-permute-start.25 = (f32[2,8,256]{2,1,0:T(8,128)S(1)}, f32[2,8,256]{2,1,0:T(8,128)S(1)}, u32[]{:S(2)}, u32[]{:S(2)}) collective-permute-start(f32[2,8,256]{2,1,0:T(8,128)S(1)} %fusion.17), channel_id=1, source_target_pairs={{0,64},{1,65},{2,66},{3,67},{8,72},{9,73},{10,74},{11,75},{16,80},... | collective-permute-start | bytes 49160 | tf_op jit(solution)/shard_map/ppermute | solution.py:34
  34.2 4.6 %collective-permute-start.26 = (f32[2,8,256]{2,1,0:T(8,128)S(1)}, f32[2,8,256]{2,1,0:T(8,128)S(1)}, u32[]{:S(2)}, u32[]{:S(2)}) collective-permute-start(f32[2,8,256]{2,1,0:T(8,128)S(1)} %fusion.17), channel_id=1, source_target_pairs={{0,128},{1,129},{2,130},{3,131},{8,136},{9,137},{10,138},{11,139},... | collective-permute-start | bytes 49160 | tf_op jit(solution)/shard_map/ppermute | solution.py:34
  34.2 4.6 %collective-permute-start.27 = (f32[2,8,256]{2,1,0:T(8,128)S(1)}, f32[2,8,256]{2,1,0:T(8,128)S(1)}, u32[]{:S(2)}, u32[]{:S(2)}) collective-permute-start(f32[2,8,256]{2,1,0:T(8,128)S(1)} %fusion.17), channel_id=1, source_target_pairs={{0,192},{1,193},{2,194},{3,195},{8,200},{9,201},{10,202},{11,203},... | collective-permute-start | bytes 49160 | tf_op jit(solution)/shard_map/ppermute | solution.py:34
  40.1 4.8 %collective-permute-start.29 = (f32[2,8,256]{2,1,0:T(8,128)S(1)}, f32[2,8,256]{2,1,0:T(8,128)S(1)}, u32[]{:S(2)}, u32[]{:S(2)}) collective-permute-start(f32[2,8,256]{2,1,0:T(8,128)S(1)} %add.228), channel_id=1, source_target_pairs={{0,48},{1,49},{2,50},{3,51},{8,56},{9,57},{10,58},{11,59},{16,0},{... | collective-permute-start | bytes 49160 | tf_op jit(solution)/shard_map/ppermute | solution.py:34
  42.6 5.2 %collective-permute-start.30 = (f32[2,8,256]{2,1,0:T(8,128)S(1)}, f32[2,8,256]{2,1,0:T(8,128)S(1)}, u32[]{:S(2)}, u32[]{:S(2)}) collective-permute-start(f32[2,8,256]{2,1,0:T(8,128)S(1)} %add.228), channel_id=1, source_target_pairs={{0,32},{1,33},{2,34},{3,35},{8,40},{9,41},{10,42},{11,43},{16,48},... | collective-permute-start | bytes 49160 | tf_op jit(solution)/shard_map/ppermute | solution.py:34
  42.6 5.2 %collective-permute-start.31 = (f32[2,8,256]{2,1,0:T(8,128)S(1)}, f32[2,8,256]{2,1,0:T(8,128)S(1)}, u32[]{:S(2)}, u32[]{:S(2)}) collective-permute-start(f32[2,8,256]{2,1,0:T(8,128)S(1)} %add.228), channel_id=1, source_target_pairs={{0,16},{1,17},{2,18},{3,19},{8,24},{9,25},{10,26},{11,27},{16,32},... | collective-permute-start | bytes 49160 | tf_op jit(solution)/shard_map/ppermute | solution.py:34
  43.7 12.1 %collective-permute-start.1 = (bf16[2,16,64,128]{3,2,1,0:T(8,128)(2,1)S(1)}, bf16[2,16,64,128]{3,2,1,0:T(8,128)(2,1)S(1)}, u32[]{:S(2)}, u32[]{:S(2)}) collective-permute-start(bf16[2,16,64,128]{3,2,1,0:T(8,128)(2,1)S(1)} %pad_maximum_fusion), channel_id=1, source_target_pairs={{0,65},{1,0},{2,130},{3,195},{8,72},{9,137},{10,11},{11,202},{16,8... | collective-permute-start | bytes 1572872 | tf_op jit(solution)/shard_map/ppermute | solution.py:34
  55.8 11.9 %collective-permute-start.2 = (bf16[2,16,64,128]{3,2,1,0:T(8,128)(2,1)S(1)}, bf16[2,16,64,128]{3,2,1,0:T(8,128)(2,1)S(1)}, u32[]{:S(2)}, u32[]{:S(2)}) collective-permute-start(bf16[2,16,64,128]{3,2,1,0:T(8,128)(2,1)S(1)} %collective-permute-done.1.refs_0_), channel_id=1, source_target_pairs={{0,16},{1,17},{2,18},{3,19},{8,57},{9,58},{10,59},{11,56},{16,32},... | collective-permute-start | bytes 1572872 | tf_op jit(solution)/shard_map/ppermute | solution.py:34
  58.1 14.4 %collective-permute-start.32 = (f32[2,32,256]{2,1,0:T(8,128)S(1)}, f32[2,32,256]{2,1,0:T(8,128)S(1)}, u32[]{:S(2)}, u32[]{:S(2)}) collective-permute-start(f32[2,32,256]{2,1,0:T(8,128)S(1)} %pad_maximum_fusion.3), channel_id=1, source_target_pairs={{0,3},{1,0},{2,1},{3,2},{4,7},{5,4},{6,5},{7,6},{8,11},{9,8},{10,9... | collective-permute-start | bytes 196616 | tf_op jit(solution)/shard_map/ppermute | solution.py:67
  61.5 24.7 %collective-permute-start.5 = (bf16[2,16,64,128]{3,2,1,0:T(8,128)(2,1)S(1)}, bf16[2,16,64,128]{3,2,1,0:T(8,128)(2,1)S(1)}, u32[]{:S(2)}, u32[]{:S(2)}) collective-permute-start(bf16[2,16,64,128]{3,2,1,0:T(8,128)(2,1)S(1)} %collective-permute-done.1.refs_0_), channel_id=1, source_target_pairs={{0,3},{1,0},{2,1},{3,2},{8,9},{9,10},{10,11},{11,8},{16,19},{17,16... | collective-permute-start | bytes 1572872 | tf_op jit(solution)/shard_map/ppermute | solution.py:34
  62.8 23.4 %collective-permute-start.7 = (bf16[2,16,64,128]{3,2,1,0:T(8,128)(2,1)S(1)}, bf16[2,16,64,128]{3,2,1,0:T(8,128)(2,1)S(1)}, u32[]{:S(2)}, u32[]{:S(2)}) collective-permute-start(bf16[2,16,64,128]{3,2,1,0:T(8,128)(2,1)S(1)} %collective-permute-done.1.refs_0_), channel_id=1, source_target_pairs={{0,48},{1,49},{2,50},{3,51},{8,25},{9,26},{10,27},{11,24},{16,3},{... | collective-permute-start | bytes 1572872 | tf_op jit(solution)/shard_map/ppermute | solution.py:34
  67.6 19.1 %collective-permute-start.3 = (bf16[2,16,64,128]{3,2,1,0:T(8,128)(2,1)S(1)}, bf16[2,16,64,128]{3,2,1,0:T(8,128)(2,1)S(1)}, u32[]{:S(2)}, u32[]{:S(2)}) collective-permute-start(bf16[2,16,64,128]{3,2,1,0:T(8,128)(2,1)S(1)} %collective-permute-done.2.refs_2_), channel_id=1, source_target_pairs={{0,16},{1,17},{2,18},{3,19},{8,57},{9,58},{10,59},{11,56},{16,32},... | collective-permute-start | bytes 1572872 | tf_op jit(solution)/shard_map/ppermute | solution.py:34
  68.7 7.4 %collective-permute-start.33 = (f32[2,32,256]{2,1,0:T(8,128)S(1)}, f32[2,32,256]{2,1,0:T(8,128)S(1)}, u32[]{:S(2)}, u32[]{:S(2)}) collective-permute-start(f32[2,32,256]{2,1,0:T(8,128)S(1)} %pad_maximum_fusion.3), channel_id=1, source_target_pairs={{0,2},{1,3},{2,0},{3,1},{4,6},{5,7},{6,4},{7,5},{8,10},{9,11},{10,... | collective-permute-start | bytes 196616 | tf_op jit(solution)/shard_map/ppermute | solution.py:67
  72.5 11.4 %collective-permute-start.34 = (f32[2,32,256]{2,1,0:T(8,128)S(1)}, f32[2,32,256]{2,1,0:T(8,128)S(1)}, u32[]{:S(2)}, u32[]{:S(2)}) collective-permute-start(f32[2,32,256]{2,1,0:T(8,128)S(1)} %pad_maximum_fusion.3), channel_id=1, source_target_pairs={{0,1},{1,2},{2,3},{3,0},{4,5},{5,6},{6,7},{7,4},{8,9},{9,10},{10,1... | collective-permute-start | bytes 196616 | tf_op jit(solution)/shard_map/ppermute | solution.py:67
  76.1 10.8 %collective-permute-start.10 = (bf16[2,16,64,128]{3,2,1,0:T(8,128)(2,1)S(1)}, bf16[2,16,64,128]{3,2,1,0:T(8,128)(2,1)S(1)}, u32[]{:S(2)}, u32[]{:S(2)}) collective-permute-start(bf16[2,16,64,128]{3,2,1,0:T(8,128)(2,1)S(1)} %collective-permute-done.1.refs_0_), channel_id=1, source_target_pairs={{0,8},{1,9},{2,10},{3,11},{8,0},{9,1},{10,2},{11,3},{16,24},{17,25... | collective-permute-start | bytes 1572872 | tf_op jit(solution)/shard_map/ppermute | solution.py:34
  83.9 5.3 %collective-permute-start.9 = (bf16[2,16,64,128]{3,2,1,0:T(8,128)(2,1)S(1)}, bf16[2,16,64,128]{3,2,1,0:T(8,128)(2,1)S(1)}, u32[]{:S(2)}, u32[]{:S(2)}) collective-permute-start(bf16[2,16,64,128]{3,2,1,0:T(8,128)(2,1)S(1)} %collective-permute-done.2.refs_2_), channel_id=1, source_target_pairs={{0,8},{1,9},{2,10},{3,11},{8,0},{9,1},{10,2},{11,3},{16,24},{17,25... | collective-permute-start | bytes 1572872 | tf_op jit(solution)/shard_map/ppermute | solution.py:34
  86.7 14.0 %collective-permute-start.4 = (bf16[2,16,64,128]{3,2,1,0:T(8,128)(2,1)S(1)}, bf16[2,16,64,128]{3,2,1,0:T(8,128)(2,1)S(1)}, u32[]{:S(2)}, u32[]{:S(2)}) collective-permute-start(bf16[2,16,64,128]{3,2,1,0:T(8,128)(2,1)S(1)} %collective-permute-done.3.refs_0_), channel_id=1, source_target_pairs={{0,8},{1,9},{2,10},{3,11},{8,0},{9,1},{10,2},{11,3},{16,24},{17,25... | collective-permute-start | bytes 1572872 | tf_op jit(solution)/shard_map/ppermute | solution.py:34
  106.3 9.4 %collective-permute-start.11 = (bf16[4,128,128]{2,1,0:T(8,128)(2,1)S(1)}, bf16[4,128,128]{2,1,0:T(8,128)(2,1)S(1)}, u32[]{:S(2)}, u32[]{:S(2)}) collective-permute-start(bf16[4,128,128]{2,1,0:T(8,128)(2,1)S(1)} %get-tuple-element.11), channel_id=1, source_target_pairs={{0,1},{1,2},{2,3},{3,0},{4,5},{5,6},{6,7},{7,4},{8,9},{9,10},{10,1... | collective-permute-start | bytes 393224 | tf_op jit(solution)/shard_map/ppermute | solution.py:67
  106.4 9.3 %collective-permute-start.12 = (bf16[4,128,128]{2,1,0:T(8,128)(2,1)S(1)}, bf16[4,128,128]{2,1,0:T(8,128)(2,1)S(1)}, u32[]{:S(2)}, u32[]{:S(2)}) collective-permute-start(bf16[4,128,128]{2,1,0:T(8,128)(2,1)S(1)} %get-tuple-element.12), channel_id=1, source_target_pairs={{0,2},{1,3},{2,0},{3,1},{4,6},{5,7},{6,4},{7,5},{8,10},{9,11},{10,... | collective-permute-start | bytes 393224 | tf_op jit(solution)/shard_map/ppermute | solution.py:67
  108.9 7.7 %collective-permute-start.13 = (bf16[4,128,128]{2,1,0:T(8,128)(2,1)S(1)}, bf16[4,128,128]{2,1,0:T(8,128)(2,1)S(1)}, u32[]{:S(2)}, u32[]{:S(2)}) collective-permute-start(bf16[4,128,128]{2,1,0:T(8,128)(2,1)S(1)} %get-tuple-element.13), channel_id=1, source_target_pairs={{0,3},{1,0},{2,1},{3,2},{4,7},{5,4},{6,5},{7,6},{8,11},{9,8},{10,9... | collective-permute-start | bytes 393224 | tf_op jit(solution)/shard_map/ppermute | solution.py:67
  116.7 12.6 %collective-permute-start.14 = (bf16[4,128,128]{2,1,0:T(8,128)(2,1)S(1)}, bf16[4,128,128]{2,1,0:T(8,128)(2,1)S(1)}, u32[]{:S(2)}, u32[]{:S(2)}) collective-permute-start(bf16[4,128,128]{2,1,0:T(8,128)(2,1)S(1)} %add_convert_fusion.mine), channel_id=1, source_target_pairs={{0,4},{4,0},{1,5},{5,1},{2,6},{6,2},{3,7},{7,3},{8,12},{12,8},{9,1... | collective-permute-start | bytes 393224 | tf_op jit(solution)/shard_map/ppermute | solution.py:71
  129.6 8.4 %collective-permute-start.16 = (bf16[512,128]{1,0:T(8,128)(2,1)S(1)}, bf16[512,128]{1,0:T(8,128)(2,1)S(1)}, u32[]{:S(2)}, u32[]{:S(2)}) collective-permute-start(bf16[512,128]{1,0:T(8,128)(2,1)S(1)} %finish.1), channel_id=1, source_target_pairs={{0,3},{1,0},{2,1},{3,2},{4,7},{5,4},{6,5},{7,6},{8,11},{9,8},{10,9... | collective-permute-start | bytes 393224 | tf_op jit(solution)/shard_map/ppermute | solution.py:67
  134.0 6.6 %collective-permute-start.17 = (bf16[512,128]{1,0:T(8,128)(2,1)S(1)}, bf16[512,128]{1,0:T(8,128)(2,1)S(1)}, u32[]{:S(2)}, u32[]{:S(2)}) collective-permute-start(bf16[512,128]{1,0:T(8,128)(2,1)S(1)} %finish.1), channel_id=1, source_target_pairs={{0,2},{1,3},{2,0},{3,1},{4,6},{5,7},{6,4},{7,5},{8,10},{9,11},{10,... | collective-permute-start | bytes 393224 | tf_op jit(solution)/shard_map/ppermute | solution.py:67
  134.6 7.2 %collective-permute-start.18 = (bf16[512,128]{1,0:T(8,128)(2,1)S(1)}, bf16[512,128]{1,0:T(8,128)(2,1)S(1)}, u32[]{:S(2)}, u32[]{:S(2)}) collective-permute-start(bf16[512,128]{1,0:T(8,128)(2,1)S(1)} %finish.1), channel_id=1, source_target_pairs={{0,1},{1,2},{2,3},{3,0},{4,5},{5,6},{6,7},{7,4},{8,9},{9,10},{10,1... | collective-permute-start | bytes 393224 | tf_op jit(solution)/shard_map/ppermute | solution.py:67
  (14 other events, 264.3 us)

commit v2 on v1

v2 whole, which is shorter than its diff:
```python
import functools
import math

import jax
import jax.numpy as jnp
from jax import lax
from jax.experimental import pallas as pl
from jax.experimental.pallas import tpu as pltpu
from jax.sharding import PartitionSpec as P

NZ, NY, NC, NR = 4, 4, 2, 4
BLK = NZ * NY * NC
TILE = 128
NT = 16
HALF = 64
BF = jnp.bfloat16
F32 = jnp.float32
VMEM = pl.BlockSpec(memory_space=pltpu.VMEM)
SMEM = pl.BlockSpec(memory_space=pltpu.SMEM)
HBM = pl.BlockSpec(memory_space=pltpu.HBM)


def place(z, y, core):
    return ((z % NZ) * NY + y % NY) * NC + core


def send(x, move):
    route = []
    for b in range(BLK):
        z, y, core = b // (NY * NC), b // NC % NY, b % NC
        for r in range(NR):
            z2, y2, core2, r2 = move(z, y, core, r)
            route.append((b * NR + r, place(z2, y2, core2) * NR + r2 % NR))
    return lax.ppermute(x, ("blk", "rep"), route)


def to_core(z, y, core, r):
    return z, y, 1 - core, r


def to_row(z, y, core, r):
    if core == 0:
        dz, to = ((1, 1), (0, 0), (2, 2), (-1, 3))[r]
    else:
        dz, to = ((1, 0), (2, 1), (0, 3), (-1, 2))[r]
    return z + dz, y, core, to


def along(steps):
    def move(z, y, core, r):
        if core == 0:
            return z, y + steps, core, r if y + steps < NY else r - 1
        return z, y - steps, core, r if y >= steps else r + 1

    return move


def send_rep(x, s):
    return lax.ppermute(x, "rep", [(r, (r + s) % NR) for r in range(NR)])


def send_col(x):
    return lax.ppermute(x, "col", [(0, 1), (1, 0)])


def sds(shape, dtype):
    return jax.ShapeDtypeStruct(shape, dtype)


def params(mib=40):
    return pltpu.CompilerParams(vmem_limit_bytes=mib << 20)


def cost(flops, nbytes):
    return pl.CostEstimate(flops=flops, bytes_accessed=nbytes, transcendentals=0)


PARTS = 4


def prep_kernel(ids, g, deg, keep, give, g_buf, deg_buf, sems):
    flip = ids[0] == 1
    count = NT // PARTS
    copies = [
        pltpu.make_async_copy(
            g.at[pl.ds(i * count, count)], g_buf.at[pl.ds(i * count, count)], sems.at[i]
        )
        for i in range(PARTS)
    ]
    copies.insert(0, pltpu.make_async_copy(deg, deg_buf, sems.at[PARTS]))
    for c in copies:
        c.start()
    copies[0].wait()
    for t in range(NT):
        if t % count == 0:
            copies[1 + t // count].wait()
        scale = 1.0 / deg_buf[pl.ds(t, 1), :].astype(F32)
        turned = (jnp.transpose(g_buf[t].astype(F32)) * scale).astype(BF)
        low, high = turned[:HALF], turned[HALF:]
        keep[t] = jnp.where(flip, high, low)
        give[t] = jnp.where(flip, low, high)


def prep(ids, g, deg):
    half = sds((NT, HALF, TILE), BF)
    g, deg = (pltpu.with_memory_space_constraint(x, pltpu.HBM) for x in (g, deg))
    return pl.pallas_call(
        prep_kernel,
        out_shape=(half, half),
        in_specs=[SMEM, HBM, HBM],
        out_specs=(VMEM, VMEM),
        scratch_shapes=[
            pltpu.VMEM((NT, TILE, TILE), BF),
            pltpu.VMEM((NT, TILE), jnp.int32),
            pltpu.SemaphoreType.DMA((PARTS + 1,)),
        ],
        compiler_params=params(8),
        cost_estimate=cost(1 << 20, 1 << 20),
        name="prep",
    )(ids, g, deg)


GROUP = 4


def spmm_kernel(items, last, base, table, tv, *refs):
    n = len(items)
    arrays = 2 * (1 + max(k for k, _ in items))
    sources, refs = refs[:arrays], refs[arrays:]
    *refs, acc, tiles, sems = refs
    distances, slots = tv.shape[1:3]
    plan = [table[distances, base + i] for i in range(n)]
    which = [jnp.maximum(p, 0) for p in plan]
    live = [jnp.where(p >= 0, jnp.clip(table[w, 2 * slots], 0, slots), 0) for p, w in zip(plan, which)]
    groups = [(x + (GROUP - 1)) >> 2 for x in live]

    def copy(i, g):
        part = pl.ds(g * GROUP, GROUP)
        return pltpu.make_async_copy(tv.at[0, which[i], part], tiles.at[i, part], sems.at[i, g])

    for i in range(n):

        @pl.loop(0, groups[i])
        def _(g, i=i):
            copy(i, g).start()

    if last:
        before, own, *outs = refs
        acc[pl.ds(0, NT)] = before[...]
    else:
        (result,) = refs
        acc[...] = jnp.zeros_like(acc)
    for i, (k, parity) in enumerate(items):
        mine, theirs = sources[2 * k], sources[2 * k + 1]

        @pl.loop(0, groups[i])
        def _(g, i=i, mine=mine, theirs=theirs, parity=parity):
            copy(i, g).wait()
            products, targets = [], []
            for u in range(GROUP):
                t = g * GROUP + u
                row = table[which[i], t]
                source = jnp.concatenate([mine[parity, row], theirs[1 - parity, row]], axis=0)
                products.append(jnp.dot(source, tiles[i, t], preferred_element_type=F32))
                targets.append(jnp.where(t < live[i], table[which[i], slots + t], NT))
            for target, product in zip(targets, products):
                acc[target] += product

    if last:
        me = table[distances, 0]
        q = NT // NR
        for i in range(q):
            own[i] = acc[me * q + i]
            for s in range(1, NR):
                to = (me + s) % NR
                outs[s - 1][i] = acc[to * q + i].astype(BF)
    else:
        result[...] = acc[pl.ds(0, NT)]


def spmm(table, base, tv, items, pairs, *more):
    last = len(more) > 0
    flat = [x for pair in pairs for x in pair]
    q, n, slots = NT // NR, len(items), tv.shape[2]
    if last:
        out_shape = (sds((q, TILE, TILE), F32),) + (sds((q, TILE, TILE), BF),) * 3
        out_specs = (VMEM,) * 4
    else:
        out_shape, out_specs = sds((NT, TILE, TILE), F32), VMEM
    return pl.pallas_call(
        functools.partial(spmm_kernel, items, last, base),
        out_shape=out_shape,
        in_specs=[SMEM, HBM] + [VMEM] * (len(flat) + len(more)),
        out_specs=out_specs,
        scratch_shapes=[
            pltpu.VMEM((NT + 1, TILE, TILE), F32),
            pltpu.VMEM((n, slots, TILE, TILE), BF),
            pltpu.SemaphoreType.DMA((n, slots // GROUP)),
        ],
        compiler_params=params(4 + 4 * n // 3),
        cost_estimate=cost(n * 10 * 2 * TILE**3, n << 20),
        name="tiles",
    )(table, tv, *flat, *more)


def finish_kernel(scale, mine, theirs, wn, self_term, extra, out):
    out[pl.ds(self_term.shape[0], TILE), :] = (extra[...] * scale).astype(BF)
    for t in range(NT // NR):
        y = jnp.concatenate([mine[t], theirs[t]], axis=0)
        turned = jnp.dot(wn[...], y, preferred_element_type=F32)
        rows = pl.ds(t * TILE, TILE)
        out[rows, :] = (self_term[rows, :] + jnp.transpose(turned)).astype(BF)


def finish(mine, theirs, wn, self_term, extra, scale):
    return pl.pallas_call(
        functools.partial(finish_kernel, scale),
        out_shape=sds((self_term.shape[0] + TILE, TILE), BF),
        in_specs=[VMEM] * 5,
        out_specs=VMEM,
        compiler_params=params(8),
        cost_estimate=cost(2 * 512 * 256 * 128, 1 << 19),
        name="finish",
    )(mine, theirs, wn, self_term, extra)


def in_order(parts, me, axis):
    n = len(parts)
    slots = jnp.stack(parts[::-1] * 2)
    at = (n - 1 - me) % n
    return jnp.concatenate(
        [
            lax.dynamic_index_in_dim(slots, at + i, 0, keepdims=False)
            for i in range(n)
        ],
        axis=axis,
    )


def after(x, *others):
    return lax.optimization_barrier((x,) + others)[0]


def sum_four(x, axis, mark):
    if axis == "y":
        got = [send(x, lambda z, y, core, r, m=m: (z, y ^ m, core, r)) for m in (1, 2, 3)]
    else:
        got = [send(x, lambda z, y, core, r, m=m: (z ^ m, y, core, r)) for m in (1, 2, 3)]
    got = lax.optimization_barrier((*got, mark))
    return (x + got[0]) + (got[1] + got[2])


def shards(
    feats, agg_feats, grad_out, w_self, w_neigh, degree, tile_vals, tile_rows, tile_cols, tile_count
):
    blk, rep, col = (lax.axis_index(a) for a in ("blk", "rep", "col"))
    core = blk % NC
    ids = jnp.stack([core, rep]).astype(jnp.int32)
    row_count, width = feats.shape
    quarter = row_count // NR

    keep, give = prep(ids, grad_out.reshape(NT, TILE, width), degree.reshape(NT, TILE))
    held = jnp.stack([keep, send(give, to_core)])
    near = send(held, to_row)
    tv = pltpu.with_memory_space_constraint(tile_vals, pltpu.HBM)
    outer = [((0, 0), 0, -1), ((3, 0), -1, 0), ((3, 1), 7, 1)]
    outer += [((1, 0), 2, 6), ((1, 1), 1, 7), ((2, 0), 6, 2), ((2, 1), 5, 3)]
    inner = [((0, 0), 4, 4), ((0, 1), 3, 5)]
    at = [rep] + [jnp.where(core == 0, a, b) for _, a, b in outer + inner]
    table = jnp.concatenate([tile_rows[0], tile_cols[0], tile_count.reshape(-1, 1)], axis=1)
    plan = jnp.pad(jnp.stack(at).astype(jnp.int32), (0, table.shape[1] - len(at)))
    table = after(jnp.concatenate([table, plan[None]], axis=0), held)
    own_first = [jnp.where(col == 0, w_neigh[:, i : i + HALF], w_neigh[:, width + i : width + i + HALF]) for i in (0, HALF)]
    other = [jnp.where(col == 0, w_neigh[:, width + i : width + i + HALF], w_neigh[:, i : i + HALF]) for i in (0, HALF)]
    turn = lambda pair: [jnp.where(core == 0, *pair), jnp.where(core == 0, *pair[::-1])]
    wn = jnp.concatenate(turn(own_first) + turn(other), axis=1)
    rows = lambda x: lax.dynamic_slice_in_dim(x, rep * quarter, quarter, 0)
    g_own = after(rows(grad_out), held)
    near, table, wn, g_own = lax.optimization_barrier((near, table, wn, g_own))
    step1 = send(near, along(1))
    step3 = send(near, along(3))
    far = send(near, lambda z, y, core, r: (z, y, core, r - 1 if core == 0 else r + 1))
    step2 = send(step1, along(1))
    near_x, step1_x, step3_x, far_x = (send(x, to_core) for x in (near, step1, step3, far))
    pairs = [(near, far_x), (step1, step3_x), (step3, step1_x), (far, near_x)]
    items = lambda plan: [i for i, _, _ in plan]
    g_other = send_col(g_own)
    g_other = after(g_other, step1, step3, far)
    g_rows = jnp.where(
        col == 0,
        jnp.concatenate([g_own, g_other], axis=1),
        jnp.concatenate([g_other, g_own], axis=1),
    )
    self_term = lax.dot_general(
        g_rows, w_self, (((1,), (1,)), ((), ())), preferred_element_type=F32
    )
    over_rows = (((0,), (0,)), ((), ()))
    partial = jnp.stack(
        [
            lax.dot_general(rows(x), g_rows, over_rows, preferred_element_type=F32)
            for x in (feats, agg_feats)
        ]
    )
    rows_each = partial.shape[1] // NR
    for_rep = lambda s: lax.dynamic_slice_in_dim(partial, (rep + s) % NR * rows_each, rows_each, 1)
    step2, *parts = lax.optimization_barrier((step2, *(for_rep(s) for s in range(NR))))
    step2_x = send(step2, to_core)
    acc = spmm(table, 1, tv, items(outer), pairs)
    got = [send_rep(parts[s], s) for s in range(1, NR)]
    piece = parts[0] + sum(lax.optimization_barrier((*got, acc))[:-1])
    piece = piece + send(piece, to_core)

    own, *outs = spmm(table, 1 + len(outer), tv, items(inner), [(step2, step2_x)], acc)
    total = own + sum(send_rep(x, s).astype(F32) for s, x in enumerate(outs, 1))
    mine = total.astype(BF)
    theirs = send_col(mine)
    piece = sum_four(after(piece, own), "z", mine)
    piece = sum_four(piece, "y", theirs).reshape(TILE, TILE)
    scale = 1.0 / math.sqrt(row_count * lax.axis_size("blk"))
    block = finish(mine, theirs, wn, self_term, piece, scale)
    blocks = [block] + [send_rep(block, s) for s in range(1, NR)]
    grad_feats = in_order([x[:quarter] for x in blocks], rep, 0)
    pieces = [x[quarter:].reshape(2, -1, 256).astype(F32) for x in blocks]
    return (grad_feats, in_order(pieces, rep, 1))


def solution(mesh):
    placed = (
        P("blk", "col"),
        P("blk", "col"),
        P("blk", "col"),
        P("col", None),
        P("col", None),
        P("blk"),
        P("blk", "rep", None, None, None),
        P("blk", "rep", None),
        P("blk", "rep", None),
        P("blk", "rep"),
    )
    return jax.shard_map(
        shards,
        mesh=mesh,
        in_specs=placed,
        out_specs=(P("blk", "col"), P(None, "col", None)),
        check_vma=False,
    )
```

time: 143 us -> 109 us (0.76)
  starting transfers between devices: 67.5 us -> 49.5 us
  local copies, waits for them, and re-layouts: 13.1 us -> 2.11 us
  waiting for transfers between devices: 47.8 us -> 39.5 us
  Pallas kernels: 8.05 us -> 10.7 us
    unnamed x42 -> x18, local copies, waits for them, and re-layouts: 11.9 us -> 0.18 us
    ppermute x12 -> x9, starting transfers between devices: 25.8 us -> 14.5 us  [send_rep(): return lax.ppermute(x, 'rep', [(r, (r + s) % NR) for r in range(NR)])]
    ppermute x12 -> x9, waiting for transfers between devices: 12.5 us -> 6.56 us  [send_rep(): return lax.ppermute(x, 'rep', [(r, (r + s) % NR) for r in range(NR)])]
    ppermute x2, starting transfers between devices: 12.4 us -> 6.78 us  [send_col(): return lax.ppermute(x, 'col', [(0, 1), (1, 0)])]
    pallas_call x4, Pallas kernels: 8.05 us -> 10.7 us  [the longest x2 8.39 us: spmm(): pl.pallas_call(functools.partial(spmm_kernel, items, last, base), out_sha...]
    ppermute x21 -> x18, waiting for transfers between devices: 22.3 us -> 20.9 us  [send(): return lax.ppermute(x, ('blk', 'rep'), route)]
    ppermute x21 -> x18, starting transfers between devices: 29.3 us -> 28.1 us  [send(): return lax.ppermute(x, ('blk', 'rep'), route)]
  transfers between devices with their start and end apart: 35 -> 29, of which waited for: 16 -> 13; matrix products, arithmetic and copies ran while one was open for 2% -> 5% of each run, Pallas kernels for 4% -> 5%
where the time goes in v2:
time: 109 us; the launch traced here: 108 us
  starting transfers between devices  49.5 us (45%)
  waiting for transfers between devices  39.5 us (36%)
  Pallas kernels  10.7 us (10%)
  other arithmetic  3.69 us (3%)
  local copies, waits for them, and re-layouts  2.11 us (2%)
  matrix products  1.58 us (1%)
    ppermute x18, starting transfers between devices, send(): return lax.ppermute(x, ('blk', 'rep'), route)  28.1 us
    ppermute x18, waiting for transfers between devices, send(): return lax.ppermute(x, ('blk', 'rep'), route)  20.9 us
    ppermute x9, starting transfers between devices, send_rep(): return lax.ppermute(x, 'rep', [(r, (r + s) % NR) for r in range(NR)])  14.5 us
    ppermute x2, waiting for transfers between devices, send_col(): return lax.ppermute(x, 'col', [(0, 1), (1, 0)])  12 us
    pallas_call x2, Pallas kernels, spmm(): pl.pallas_call(functools.partial(spmm_kernel, items, last, base), out_sha...  8.39 us
    ppermute x2, starting transfers between devices, send_col(): return lax.ppermute(x, 'col', [(0, 1), (1, 0)])  6.78 us
    ppermute x9, waiting for transfers between devices, send_rep(): return lax.ppermute(x, 'rep', [(r, (r + s) % NR) for r in range(NR)])  6.56 us
  transfers between devices with their start and end apart: 29, of which 13 were waited for; matrix products, arithmetic and copies ran while one was open for 5% of the time, Pallas kernels for 5%

profile of v2, /device:TPU:32, one launch (start us, length us, event | category | flops | bytes accessed | tf_op | source)
XLA Modules:
  0.0 108.0 jit_solution(11997125591596076569)
XLA Ops:
  0.7 2.0 %prep.1 = (bf16[16,64,128]{2,1,0:T(8,128)(2,1)S(1)}, bf16[16,64,128]{2,1,0:T(8,128)(2,1)S(1)}) custom-call(s32[2]{0:T(128)S(1)} %pad_add_fusion.1.ids, bf16[16,128,128]{2,1,0:T(8,128)(2,1)} %bitcast.65, s32[16,128]{1,0:T(8,128)} %bitcast.67), custom_call_target="tpu_custom_call" | custom-call | flops 1048576 | bytes 1048576 | tf_op jit(solution)/shard_map/prep/pallas_call | solution.py:107
  4.4 2.9 %collective-permute-start.1 = (bf16[2,16,64,128]{3,2,1,0:T(8,128)(2,1)S(1)}, bf16[2,16,64,128]{3,2,1,0:T(8,128)(2,1)S(1)}, u32[]{:S(2)}, u32[]{:S(2)}) collective-permute-start(bf16[2,16,64,128]{3,2,1,0:T(8,128)(2,1)S(1)} %pad_maximum_fusion), channel_id=1, source_target_pairs={{0,65},{1,0},{2,130},{3,195},{8,72},{9,137},{10,11},{11,202},{16,8... | collective-permute-start | bytes 1572872 | tf_op jit(solution)/shard_map/ppermute | solution.py:34
  10.1 7.8 %collective-permute-done.1.refs_0_ = bf16[2,16,64,128]{3,2,1,0:T(8,128)(2,1)S(1)} collective-permute-done((bf16[2,16,64,128]{3,2,1,0:T(8,128)(2,1)S(1)}, bf16[2,16,64,128]{3,2,1,0:T(8,128)(2,1)S(1)}, u32[]{:S(2)}, u32[]{:S(2)}) %collective-permute-start.1) | collective-permute-done | bytes 524320 | tf_op jit(solution)/shard_map/ppermute | solution.py:34
  17.9 1.6 %collective-permute-start.2 = (bf16[2,16,64,128]{3,2,1,0:T(8,128)(2,1)S(1)}, bf16[2,16,64,128]{3,2,1,0:T(8,128)(2,1)S(1)}, u32[]{:S(2)}, u32[]{:S(2)}) collective-permute-start(bf16[2,16,64,128]{3,2,1,0:T(8,128)(2,1)S(1)} %collective-permute-done.1.refs_0_), channel_id=1, source_target_pairs={{0,16},{1,17},{2,18},{3,19},{8,57},{9,58},{10,59},{11,56},{16,32},... | collective-permute-start | bytes 1572872 | tf_op jit(solution)/shard_map/ppermute | solution.py:34
  19.5 3.6 %collective-permute-start.6 = (bf16[2,16,64,128]{3,2,1,0:T(8,128)(2,1)S(1)}, bf16[2,16,64,128]{3,2,1,0:T(8,128)(2,1)S(1)}, u32[]{:S(2)}, u32[]{:S(2)}) collective-permute-start(bf16[2,16,64,128]{3,2,1,0:T(8,128)(2,1)S(1)} %collective-permute-done.1.refs_0_), channel_id=1, source_target_pairs={{0,3},{1,0},{2,1},{3,2},{8,9},{9,10},{10,11},{11,8},{16,19},{17,16... | collective-permute-start | bytes 1572872 | tf_op jit(solution)/shard_map/ppermute | solution.py:34
  23.0 2.8 %collective-permute-start.5 = (bf16[2,16,64,128]{3,2,1,0:T(8,128)(2,1)S(1)}, bf16[2,16,64,128]{3,2,1,0:T(8,128)(2,1)S(1)}, u32[]{:S(2)}, u32[]{:S(2)}) collective-permute-start(bf16[2,16,64,128]{3,2,1,0:T(8,128)(2,1)S(1)} %collective-permute-done.1.refs_0_), channel_id=1, source_target_pairs={{0,48},{1,49},{2,50},{3,51},{8,25},{9,26},{10,27},{11,24},{16,3},{... | collective-permute-start | bytes 1572872 | tf_op jit(solution)/shard_map/ppermute | solution.py:34
  25.9 3.7 %collective-permute-done.2.refs_2_ = bf16[2,16,64,128]{3,2,1,0:T(8,128)(2,1)S(1)} collective-permute-done((bf16[2,16,64,128]{3,2,1,0:T(8,128)(2,1)S(1)}, bf16[2,16,64,128]{3,2,1,0:T(8,128)(2,1)S(1)}, u32[]{:S(2)}, u32[]{:S(2)}) %collective-permute-start.2) | collective-permute-done | bytes 524320 | tf_op jit(solution)/shard_map/ppermute | solution.py:34
  29.6 3.7 %collective-permute-start.3 = (bf16[2,16,64,128]{3,2,1,0:T(8,128)(2,1)S(1)}, bf16[2,16,64,128]{3,2,1,0:T(8,128)(2,1)S(1)}, u32[]{:S(2)}, u32[]{:S(2)}) collective-permute-start(bf16[2,16,64,128]{3,2,1,0:T(8,128)(2,1)S(1)} %collective-permute-done.2.refs_2_), channel_id=1, source_target_pairs={{0,16},{1,17},{2,18},{3,19},{8,57},{9,58},{10,59},{11,56},{16,32},... | collective-permute-start | bytes 1572872 | tf_op jit(solution)/shard_map/ppermute | solution.py:34
  33.3 2.6 %collective-permute-start.4 = (bf16[512,128]{1,0:T(8,128)(2,1)S(1)}, bf16[512,128]{1,0:T(8,128)(2,1)S(1)}, u32[]{:S(2)}, u32[]{:S(2)}) collective-permute-start(bf16[512,128]{1,0:T(8,128)(2,1)S(1)} %constant_dynamic-slice_fusion), channel_id=1, source_target_pairs={{0,4},{4,0},{1,5},{5,1},{2,6},{6,2},{3,7},{7,3},{8,12},{12,8},{9,1... | collective-permute-start | bytes 393224 | tf_op jit(solution)/shard_map/ppermute | solution.py:63
  35.9 1.6 %collective-permute-start.11 = (bf16[2,16,64,128]{3,2,1,0:T(8,128)(2,1)S(1)}, bf16[2,16,64,128]{3,2,1,0:T(8,128)(2,1)S(1)}, u32[]{:S(2)}, u32[]{:S(2)}) collective-permute-start(bf16[2,16,64,128]{3,2,1,0:T(8,128)(2,1)S(1)} %collective-permute-done.1.refs_0_), channel_id=1, source_target_pairs={{0,8},{1,9},{2,10},{3,11},{8,0},{9,1},{10,2},{11,3},{16,24},{17,25... | collective-permute-start | bytes 1572872 | tf_op jit(solution)/shard_map/ppermute | solution.py:34
  37.5 6.0 %collective-permute-done.4 = bf16[512,128]{1,0:T(8,128)(2,1)S(1)} collective-permute-done((bf16[512,128]{1,0:T(8,128)(2,1)S(1)}, bf16[512,128]{1,0:T(8,128)(2,1)S(1)}, u32[]{:S(2)}, u32[]{:S(2)}) %collective-permute-start.4) | collective-permute-done | bytes 131104 | tf_op jit(solution)/shard_map/ppermute | solution.py:63
  44.3 1.1 %convolution_bitcast_fusion.1 = f32[1,128,256]{2,1,0:T(8,128)S(1)} fusion(bf16[2048,128]{1,0:T(8,128)(2,1)} %param.10, s32[]{:T(128)S(6)} %select_n.155, bf16[512,128]{1,0:T(8,128)(2,1)S(1)} %collective-permute-done.4, bf16[512,128]{1,0:T(8,128)(2,1)S(1)} %constant_dynamic-slice_fusion, pred[]{:T(512)S(6)} %eq.13), kind=kOutput, calls=%fused_computation.1 | convolution fusion | flops 34734080 | bytes 524293 | tf_op jit(solution)/shard_map/dot_general | solution.py:300
  46.5 2.7 %collective-permute-start.16 = (f32[2,32,256]{2,1,0:T(8,128)S(1)}, f32[2,32,256]{2,1,0:T(8,128)S(1)}, u32[]{:S(2)}, u32[]{:S(2)}) collective-permute-start(f32[2,32,256]{2,1,0:T(8,128)S(1)} %get-tuple-element.45), channel_id=1, source_target_pairs={{0,1},{1,2},{2,3},{3,0},{4,5},{5,6},{6,7},{7,4},{8,9},{9,10},{10,1... | collective-permute-start | bytes 196616 | tf_op jit(solution)/shard_map/ppermute | solution.py:59
  49.1 3.2 %collective-permute-start.17 = (f32[2,32,256]{2,1,0:T(8,128)S(1)}, f32[2,32,256]{2,1,0:T(8,128)S(1)}, u32[]{:S(2)}, u32[]{:S(2)}) collective-permute-start(f32[2,32,256]{2,1,0:T(8,128)S(1)} %get-tuple-element.46), channel_id=1, source_target_pairs={{0,2},{1,3},{2,0},{3,1},{4,6},{5,7},{6,4},{7,5},{8,10},{9,11},{10,... | collective-permute-start | bytes 196616 | tf_op jit(solution)/shard_map/ppermute | solution.py:59
  52.3 1.2 %collective-permute-start.18 = (f32[2,32,256]{2,1,0:T(8,128)S(1)}, f32[2,32,256]{2,1,0:T(8,128)S(1)}, u32[]{:S(2)}, u32[]{:S(2)}) collective-permute-start(f32[2,32,256]{2,1,0:T(8,128)S(1)} %get-tuple-element.47), channel_id=1, source_target_pairs={{0,3},{1,0},{2,1},{3,2},{4,7},{5,4},{6,5},{7,6},{8,11},{9,8},{10,9... | collective-permute-start | bytes 196616 | tf_op jit(solution)/shard_map/ppermute | solution.py:59
  53.5 5.5 %tiles.2.refs_2_ = f32[16,128,128]{2,1,0:T(8,128)S(1)} custom-call(s32[9,81]{1,0:T(8,128)S(1)} %pad_add_fusion.table, bf16[1,8,40,128,128]{4,3,2,1,0:T(8,128)(2,1)} %tv.3, bf16[2,16,64,128]{3,2,1,0:T(8,128)(2,1)S(1)} %collective-permute-done.1.refs_0_, bf16[2,16,64,128]{3,2,1,0:T(8,128)(2,1)S(1)} %collective-permute-done.8.refs_1_, ...), custom_call_target="tpu_custom_call" | custom-call | flops 293601280 | bytes 7340032 | tf_op jit(solution)/shard_map/tiles/pallas_call | solution.py:190
  59.0 2.9 %tiles.3 = (f32[4,128,128]{2,1,0:T(8,128)S(1)}, bf16[4,128,128]{2,1,0:T(8,128)(2,1)S(1)}, bf16[4,128,128]{2,1,0:T(8,128)(2,1)S(1)}, bf16[4,128,128]{2,1,0:T(8,128)(2,1)S(1)}) custom-call(s32[9,81]{1,0:T(8,128)S(1)} %pad_add_fusion.table, bf16[1,8,40,128,128]{4,3,2,1,0:T(8,128)(2,1)} %tv.3, bf16[2,16,64,128]{3,2,1,0:T(8,128)(2,1)S(1)} %collective-permute-done.3.refs_0_, ...), custom_call_target="tpu_custom_call" | custom-call | flops 83886080 | bytes 2097152 | tf_op jit(solution)/shard_map/tiles/pallas_call | solution.py:190
  62.2 3.0 %collective-permute-start.13 = (bf16[4,128,128]{2,1,0:T(8,128)(2,1)S(1)}, bf16[4,128,128]{2,1,0:T(8,128)(2,1)S(1)}, u32[]{:S(2)}, u32[]{:S(2)}) collective-permute-start(bf16[4,128,128]{2,1,0:T(8,128)(2,1)S(1)} %get-tuple-element.41), channel_id=1, source_target_pairs={{0,2},{1,3},{2,0},{3,1},{4,6},{5,7},{6,4},{7,5},{8,10},{9,11},{10,... | collective-permute-start | bytes 393224 | tf_op jit(solution)/shard_map/ppermute | solution.py:59
  65.9 1.2 %collective-permute-done.19 = f32[2,32,256]{2,1,0:T(8,128)S(1)} collective-permute-done((f32[2,32,256]{2,1,0:T(8,128)S(1)}, f32[2,32,256]{2,1,0:T(8,128)S(1)}, u32[]{:S(2)}, u32[]{:S(2)}) %collective-permute-start.19) | collective-permute-done | bytes 65568 | tf_op jit(solution)/shard_map/ppermute | solution.py:34
  67.2 4.0 %collective-permute-start.20 = (f32[2,32,256]{2,1,0:T(8,128)S(1)}, f32[2,32,256]{2,1,0:T(8,128)S(1)}, u32[]{:S(2)}, u32[]{:S(2)}) collective-permute-start(f32[2,32,256]{2,1,0:T(8,128)S(1)} %add.142), channel_id=1, source_target_pairs={{0,64},{1,65},{2,66},{3,67},{8,72},{9,73},{10,74},{11,75},{16,80},... | collective-permute-start | bytes 196616 | tf_op jit(solution)/shard_map/ppermute | solution.py:34
  71.1 2.0 %collective-permute-start.21 = (f32[2,32,256]{2,1,0:T(8,128)S(1)}, f32[2,32,256]{2,1,0:T(8,128)S(1)}, u32[]{:S(2)}, u32[]{:S(2)}) collective-permute-start(f32[2,32,256]{2,1,0:T(8,128)S(1)} %add.142), channel_id=1, source_target_pairs={{0,128},{1,129},{2,130},{3,131},{8,136},{9,137},{10,138},{11,139},... | collective-permute-start | bytes 196616 | tf_op jit(solution)/shard_map/ppermute | solution.py:34
  73.8 4.4 %collective-permute-done.21 = f32[2,32,256]{2,1,0:T(8,128)S(1)} collective-permute-done((f32[2,32,256]{2,1,0:T(8,128)S(1)}, f32[2,32,256]{2,1,0:T(8,128)S(1)}, u32[]{:S(2)}, u32[]{:S(2)}) %collective-permute-start.21) | collective-permute-done | bytes 65568 | tf_op jit(solution)/shard_map/ppermute | solution.py:34
  78.2 1.9 %collective-permute-done.22 = f32[2,32,256]{2,1,0:T(8,128)S(1)} collective-permute-done((f32[2,32,256]{2,1,0:T(8,128)S(1)}, f32[2,32,256]{2,1,0:T(8,128)S(1)}, u32[]{:S(2)}, u32[]{:S(2)}) %collective-permute-start.22) | collective-permute-done | bytes 65568 | tf_op jit(solution)/shard_map/ppermute | solution.py:34
  80.1 1.2 %collective-permute-start.23 = (f32[2,32,256]{2,1,0:T(8,128)S(1)}, f32[2,32,256]{2,1,0:T(8,128)S(1)}, u32[]{:S(2)}, u32[]{:S(2)}) collective-permute-start(f32[2,32,256]{2,1,0:T(8,128)S(1)} %add_add_fusion.1), channel_id=1, source_target_pairs={{0,16},{1,17},{2,18},{3,19},{8,24},{9,25},{10,26},{11,27},{16,0},{... | collective-permute-start | bytes 196616 | tf_op jit(solution)/shard_map/ppermute | solution.py:34
  81.3 1.8 %collective-permute-start.24 = (f32[2,32,256]{2,1,0:T(8,128)S(1)}, f32[2,32,256]{2,1,0:T(8,128)S(1)}, u32[]{:S(2)}, u32[]{:S(2)}) collective-permute-start(f32[2,32,256]{2,1,0:T(8,128)S(1)} %add_add_fusion.1), channel_id=1, source_target_pairs={{0,32},{1,33},{2,34},{3,35},{8,40},{9,41},{10,42},{11,43},{16,48},... | collective-permute-start | bytes 196616 | tf_op jit(solution)/shard_map/ppermute | solution.py:34
  83.1 1.8 %collective-permute-start.25 = (f32[2,32,256]{2,1,0:T(8,128)S(1)}, f32[2,32,256]{2,1,0:T(8,128)S(1)}, u32[]{:S(2)}, u32[]{:S(2)}) collective-permute-start(f32[2,32,256]{2,1,0:T(8,128)S(1)} %add_add_fusion.1), channel_id=1, source_target_pairs={{0,48},{1,49},{2,50},{3,51},{8,56},{9,57},{10,58},{11,59},{16,32},... | collective-permute-start | bytes 196616 | tf_op jit(solution)/shard_map/ppermute | solution.py:34
  84.9 4.2 %collective-permute-start.15 = (bf16[4,128,128]{2,1,0:T(8,128)(2,1)S(1)}, bf16[4,128,128]{2,1,0:T(8,128)(2,1)S(1)}, u32[]{:S(2)}, u32[]{:S(2)}) collective-permute-start(bf16[4,128,128]{2,1,0:T(8,128)(2,1)S(1)} %add_convert_fusion.mine), channel_id=1, source_target_pairs={{0,4},{4,0},{1,5},{5,1},{2,6},{6,2},{3,7},{7,3},{8,12},{12,8},{9,1... | collective-permute-start | bytes 393224 | tf_op jit(solution)/shard_map/ppermute | solution.py:63
  89.4 6.0 %collective-permute-done.15.theirs = bf16[4,128,128]{2,1,0:T(8,128)(2,1)S(1)} collective-permute-done((bf16[4,128,128]{2,1,0:T(8,128)(2,1)S(1)}, bf16[4,128,128]{2,1,0:T(8,128)(2,1)S(1)}, u32[]{:S(2)}, u32[]{:S(2)}) %collective-permute-start.15) | collective-permute-done | bytes 131104 | tf_op jit(solution)/shard_map/ppermute | solution.py:63
  96.8 1.4 %collective-permute-start.27 = (bf16[640,128]{1,0:T(8,128)(2,1)S(1)}, bf16[640,128]{1,0:T(8,128)(2,1)S(1)}, u32[]{:S(2)}, u32[]{:S(2)}) collective-permute-start(bf16[640,128]{1,0:T(8,128)(2,1)S(1)} %finish.1), channel_id=1, source_target_pairs={{0,2},{1,3},{2,0},{3,1},{4,6},{5,7},{6,4},{7,5},{8,10},{9,11},{10,... | collective-permute-start | bytes 491528 | tf_op jit(solution)/shard_map/ppermute | solution.py:59
  99.4 2.6 %collective-permute-done.26 = bf16[640,128]{1,0:T(8,128)(2,1)S(1)} collective-permute-done((bf16[640,128]{1,0:T(8,128)(2,1)S(1)}, bf16[640,128]{1,0:T(8,128)(2,1)S(1)}, u32[]{:S(2)}, u32[]{:S(2)}) %collective-permute-start.26) | collective-permute-done | bytes 163872 | tf_op jit(solution)/shard_map/ppermute | solution.py:59
  102.0 1.7 %collective-permute-done.27 = bf16[640,128]{1,0:T(8,128)(2,1)S(1)} collective-permute-done((bf16[640,128]{1,0:T(8,128)(2,1)S(1)}, bf16[640,128]{1,0:T(8,128)(2,1)S(1)}, u32[]{:S(2)}, u32[]{:S(2)}) %collective-permute-start.27) | collective-permute-done | bytes 163872 | tf_op jit(solution)/shard_map/ppermute | solution.py:59
  103.8 2.2 %collective-permute-done.28 = bf16[640,128]{1,0:T(8,128)(2,1)S(1)} collective-permute-done((bf16[640,128]{1,0:T(8,128)(2,1)S(1)}, bf16[640,128]{1,0:T(8,128)(2,1)S(1)}, u32[]{:S(2)}, u32[]{:S(2)}) %collective-permute-start.28) | collective-permute-done | bytes 163872 | tf_op jit(solution)/shard_map/ppermute | solution.py:59
  (82 shorter events, 12.6 us)
Async XLA Ops:
  0.6 43.4 %copy-start = (bf16[2048,128]{1,0:T(8,128)(2,1)S(1)}, bf16[2048,128]{1,0:T(8,128)(2,1)}, u32[]{:S(2)}) copy-start(bf16[2048,128]{1,0:T(8,128)(2,1)} %param.11) | copy-start | bytes 1572868
  2.7 1.6 %collective-permute-start = (bf16[16,64,128]{2,1,0:T(8,128)(2,1)S(1)}, bf16[16,64,128]{2,1,0:T(8,128)(2,1)S(1)}, u32[]{:S(2)}, u32[]{:S(2)}) collective-permute-start(bf16[16,64,128]{2,1,0:T(8,128)(2,1)S(1)} %get-tuple-element.31), channel_id=1, source_target_pairs={{0,8},{1,9},{2,10},{3,11},{8,0},{9,1},{10,2},{11,3},{16,24},{17,25... | collective-permute-start | bytes 786440 | tf_op jit(solution)/shard_map/ppermute | solution.py:34
  4.4 13.5 %collective-permute-start.1 = (bf16[2,16,64,128]{3,2,1,0:T(8,128)(2,1)S(1)}, bf16[2,16,64,128]{3,2,1,0:T(8,128)(2,1)S(1)}, u32[]{:S(2)}, u32[]{:S(2)}) collective-permute-start(bf16[2,16,64,128]{3,2,1,0:T(8,128)(2,1)S(1)} %pad_maximum_fusion), channel_id=1, source_target_pairs={{0,65},{1,0},{2,130},{3,195},{8,72},{9,137},{10,11},{11,202},{16,8... | collective-permute-start | bytes 1572872 | tf_op jit(solution)/shard_map/ppermute | solution.py:34
  17.9 11.7 %collective-permute-start.2 = (bf16[2,16,64,128]{3,2,1,0:T(8,128)(2,1)S(1)}, bf16[2,16,64,128]{3,2,1,0:T(8,128)(2,1)S(1)}, u32[]{:S(2)}, u32[]{:S(2)}) collective-permute-start(bf16[2,16,64,128]{3,2,1,0:T(8,128)(2,1)S(1)} %collective-permute-done.1.refs_0_), channel_id=1, source_target_pairs={{0,16},{1,17},{2,18},{3,19},{8,57},{9,58},{10,59},{11,56},{16,32},... | collective-permute-start | bytes 1572872 | tf_op jit(solution)/shard_map/ppermute | solution.py:34
  19.5 24.0 %collective-permute-start.6 = (bf16[2,16,64,128]{3,2,1,0:T(8,128)(2,1)S(1)}, bf16[2,16,64,128]{3,2,1,0:T(8,128)(2,1)S(1)}, u32[]{:S(2)}, u32[]{:S(2)}) collective-permute-start(bf16[2,16,64,128]{3,2,1,0:T(8,128)(2,1)S(1)} %collective-permute-done.1.refs_0_), channel_id=1, source_target_pairs={{0,3},{1,0},{2,1},{3,2},{8,9},{9,10},{10,11},{11,8},{16,19},{17,16... | collective-permute-start | bytes 1572872 | tf_op jit(solution)/shard_map/ppermute | solution.py:34
  23.0 20.4 %collective-permute-start.5 = (bf16[2,16,64,128]{3,2,1,0:T(8,128)(2,1)S(1)}, bf16[2,16,64,128]{3,2,1,0:T(8,128)(2,1)S(1)}, u32[]{:S(2)}, u32[]{:S(2)}) collective-permute-start(bf16[2,16,64,128]{3,2,1,0:T(8,128)(2,1)S(1)} %collective-permute-done.1.refs_0_), channel_id=1, source_target_pairs={{0,48},{1,49},{2,50},{3,51},{8,25},{9,26},{10,27},{11,24},{16,3},{... | collective-permute-start | bytes 1572872 | tf_op jit(solution)/shard_map/ppermute | solution.py:34
  29.6 16.8 %collective-permute-start.3 = (bf16[2,16,64,128]{3,2,1,0:T(8,128)(2,1)S(1)}, bf16[2,16,64,128]{3,2,1,0:T(8,128)(2,1)S(1)}, u32[]{:S(2)}, u32[]{:S(2)}) collective-permute-start(bf16[2,16,64,128]{3,2,1,0:T(8,128)(2,1)S(1)} %collective-permute-done.2.refs_2_), channel_id=1, source_target_pairs={{0,16},{1,17},{2,18},{3,19},{8,57},{9,58},{10,59},{11,56},{16,32},... | collective-permute-start | bytes 1572872 | tf_op jit(solution)/shard_map/ppermute | solution.py:34
  33.3 10.1 %collective-permute-start.4 = (bf16[512,128]{1,0:T(8,128)(2,1)S(1)}, bf16[512,128]{1,0:T(8,128)(2,1)S(1)}, u32[]{:S(2)}, u32[]{:S(2)}) collective-permute-start(bf16[512,128]{1,0:T(8,128)(2,1)S(1)} %constant_dynamic-slice_fusion), channel_id=1, source_target_pairs={{0,4},{4,0},{1,5},{5,1},{2,6},{6,2},{3,7},{7,3},{8,12},{12,8},{9,1... | collective-permute-start | bytes 393224 | tf_op jit(solution)/shard_map/ppermute | solution.py:63
  35.9 10.5 %collective-permute-start.11 = (bf16[2,16,64,128]{3,2,1,0:T(8,128)(2,1)S(1)}, bf16[2,16,64,128]{3,2,1,0:T(8,128)(2,1)S(1)}, u32[]{:S(2)}, u32[]{:S(2)}) collective-permute-start(bf16[2,16,64,128]{3,2,1,0:T(8,128)(2,1)S(1)} %collective-permute-done.1.refs_0_), channel_id=1, source_target_pairs={{0,8},{1,9},{2,10},{3,11},{8,0},{9,1},{10,2},{11,3},{16,24},{17,25... | collective-permute-start | bytes 1572872 | tf_op jit(solution)/shard_map/ppermute | solution.py:34
  43.4 5.7 %collective-permute-start.10 = (bf16[2,16,64,128]{3,2,1,0:T(8,128)(2,1)S(1)}, bf16[2,16,64,128]{3,2,1,0:T(8,128)(2,1)S(1)}, u32[]{:S(2)}, u32[]{:S(2)}) collective-permute-start(bf16[2,16,64,128]{3,2,1,0:T(8,128)(2,1)S(1)} %collective-permute-done.2.refs_2_), channel_id=1, source_target_pairs={{0,8},{1,9},{2,10},{3,11},{8,0},{9,1},{10,2},{11,3},{16,24},{17,25... | collective-permute-start | bytes 1572872 | tf_op jit(solution)/shard_map/ppermute | solution.py:34
  43.5 8.9 %collective-permute-start.8 = (bf16[2,16,64,128]{3,2,1,0:T(8,128)(2,1)S(1)}, bf16[2,16,64,128]{3,2,1,0:T(8,128)(2,1)S(1)}, u32[]{:S(2)}, u32[]{:S(2)}) collective-permute-start(bf16[2,16,64,128]{3,2,1,0:T(8,128)(2,1)S(1)} %collective-permute-done.6.refs_6_), channel_id=1, source_target_pairs={{0,8},{1,9},{2,10},{3,11},{8,0},{9,1},{10,2},{11,3},{16,24},{17,25... | collective-permute-start | bytes 1572872 | tf_op jit(solution)/shard_map/ppermute | solution.py:34
  44.0 9.6 %collective-permute-start.9 = (bf16[2,16,64,128]{3,2,1,0:T(8,128)(2,1)S(1)}, bf16[2,16,64,128]{3,2,1,0:T(8,128)(2,1)S(1)}, u32[]{:S(2)}, u32[]{:S(2)}) collective-permute-start(bf16[2,16,64,128]{3,2,1,0:T(8,128)(2,1)S(1)} %collective-permute-done.5.refs_4_), channel_id=1, source_target_pairs={{0,8},{1,9},{2,10},{3,11},{8,0},{9,1},{10,2},{11,3},{16,24},{17,25... | collective-permute-start | bytes 1572872 | tf_op jit(solution)/shard_map/ppermute | solution.py:34
  46.4 12.6 %collective-permute-start.7 = (bf16[2,16,64,128]{3,2,1,0:T(8,128)(2,1)S(1)}, bf16[2,16,64,128]{3,2,1,0:T(8,128)(2,1)S(1)}, u32[]{:S(2)}, u32[]{:S(2)}) collective-permute-start(bf16[2,16,64,128]{3,2,1,0:T(8,128)(2,1)S(1)} %collective-permute-done.3.refs_0_), channel_id=1, source_target_pairs={{0,8},{1,9},{2,10},{3,11},{8,0},{9,1},{10,2},{11,3},{16,24},{17,25... | collective-permute-start | bytes 1572872 | tf_op jit(solution)/shard_map/ppermute | solution.py:34
  46.5 12.5 %collective-permute-start.16 = (f32[2,32,256]{2,1,0:T(8,128)S(1)}, f32[2,32,256]{2,1,0:T(8,128)S(1)}, u32[]{:S(2)}, u32[]{:S(2)}) collective-permute-start(f32[2,32,256]{2,1,0:T(8,128)S(1)} %get-tuple-element.45), channel_id=1, source_target_pairs={{0,1},{1,2},{2,3},{3,0},{4,5},{5,6},{6,7},{7,4},{8,9},{9,10},{10,1... | collective-permute-start | bytes 196616 | tf_op jit(solution)/shard_map/ppermute | solution.py:59
  49.1 9.9 %collective-permute-start.17 = (f32[2,32,256]{2,1,0:T(8,128)S(1)}, f32[2,32,256]{2,1,0:T(8,128)S(1)}, u32[]{:S(2)}, u32[]{:S(2)}) collective-permute-start(f32[2,32,256]{2,1,0:T(8,128)S(1)} %get-tuple-element.46), channel_id=1, source_target_pairs={{0,2},{1,3},{2,0},{3,1},{4,6},{5,7},{6,4},{7,5},{8,10},{9,11},{10,... | collective-permute-start | bytes 196616 | tf_op jit(solution)/shard_map/ppermute | solution.py:59
  52.3 6.7 %collective-permute-start.18 = (f32[2,32,256]{2,1,0:T(8,128)S(1)}, f32[2,32,256]{2,1,0:T(8,128)S(1)}, u32[]{:S(2)}, u32[]{:S(2)}) collective-permute-start(f32[2,32,256]{2,1,0:T(8,128)S(1)} %get-tuple-element.47), channel_id=1, source_target_pairs={{0,3},{1,0},{2,1},{3,2},{4,7},{5,4},{6,5},{7,6},{8,11},{9,8},{10,9... | collective-permute-start | bytes 196616 | tf_op jit(solution)/shard_map/ppermute | solution.py:59
  59.0 30.1 %copy-start.1 = (bf16[128,256]{1,0:T(8,128)(2,1)S(1)}, bf16[128,256]{1,0:T(8,128)(2,1)}, u32[]{:S(2)}) copy-start(bf16[128,256]{1,0:T(8,128)(2,1)} %param.13) | copy-start | bytes 196612
  62.0 11.1 %collective-permute-start.12 = (bf16[4,128,128]{2,1,0:T(8,128)(2,1)S(1)}, bf16[4,128,128]{2,1,0:T(8,128)(2,1)S(1)}, u32[]{:S(2)}, u32[]{:S(2)}) collective-permute-start(bf16[4,128,128]{2,1,0:T(8,128)(2,1)S(1)} %get-tuple-element.40), channel_id=1, source_target_pairs={{0,1},{1,2},{2,3},{3,0},{4,5},{5,6},{6,7},{7,4},{8,9},{9,10},{10,1... | collective-permute-start | bytes 393224 | tf_op jit(solution)/shard_map/ppermute | solution.py:59
  62.2 11.4 %collective-permute-start.13 = (bf16[4,128,128]{2,1,0:T(8,128)(2,1)S(1)}, bf16[4,128,128]{2,1,0:T(8,128)(2,1)S(1)}, u32[]{:S(2)}, u32[]{:S(2)}) collective-permute-start(bf16[4,128,128]{2,1,0:T(8,128)(2,1)S(1)} %get-tuple-element.41), channel_id=1, source_target_pairs={{0,2},{1,3},{2,0},{3,1},{4,6},{5,7},{6,4},{7,5},{8,10},{9,11},{10,... | collective-permute-start | bytes 393224 | tf_op jit(solution)/shard_map/ppermute | solution.py:59
  65.1 8.4 %collective-permute-start.14 = (bf16[4,128,128]{2,1,0:T(8,128)(2,1)S(1)}, bf16[4,128,128]{2,1,0:T(8,128)(2,1)S(1)}, u32[]{:S(2)}, u32[]{:S(2)}) collective-permute-start(bf16[4,128,128]{2,1,0:T(8,128)(2,1)S(1)} %get-tuple-element.42), channel_id=1, source_target_pairs={{0,3},{1,0},{2,1},{3,2},{4,7},{5,4},{6,5},{7,6},{8,11},{9,8},{10,9... | collective-permute-start | bytes 393224 | tf_op jit(solution)/shard_map/ppermute | solution.py:59
  65.8 1.3 %collective-permute-start.19 = (f32[2,32,256]{2,1,0:T(8,128)S(1)}, f32[2,32,256]{2,1,0:T(8,128)S(1)}, u32[]{:S(2)}, u32[]{:S(2)}) collective-permute-start(f32[2,32,256]{2,1,0:T(8,128)S(1)} %add_add_fusion.2), channel_id=1, source_target_pairs={{0,8},{1,9},{2,10},{3,11},{8,0},{9,1},{10,2},{11,3},{16,24},{17,25... | collective-permute-start | bytes 196616 | tf_op jit(solution)/shard_map/ppermute | solution.py:34
  67.2 6.6 %collective-permute-start.20 = (f32[2,32,256]{2,1,0:T(8,128)S(1)}, f32[2,32,256]{2,1,0:T(8,128)S(1)}, u32[]{:S(2)}, u32[]{:S(2)}) collective-permute-start(f32[2,32,256]{2,1,0:T(8,128)S(1)} %add.142), channel_id=1, source_target_pairs={{0,64},{1,65},{2,66},{3,67},{8,72},{9,73},{10,74},{11,75},{16,80},... | collective-permute-start | bytes 196616 | tf_op jit(solution)/shard_map/ppermute | solution.py:34
  71.1 7.0 %collective-permute-start.21 = (f32[2,32,256]{2,1,0:T(8,128)S(1)}, f32[2,32,256]{2,1,0:T(8,128)S(1)}, u32[]{:S(2)}, u32[]{:S(2)}) collective-permute-start(f32[2,32,256]{2,1,0:T(8,128)S(1)} %add.142), channel_id=1, source_target_pairs={{0,128},{1,129},{2,130},{3,131},{8,136},{9,137},{10,138},{11,139},... | collective-permute-start | bytes 196616 | tf_op jit(solution)/shard_map/ppermute | solution.py:34
  73.1 7.0 %collective-permute-start.22 = (f32[2,32,256]{2,1,0:T(8,128)S(1)}, f32[2,32,256]{2,1,0:T(8,128)S(1)}, u32[]{:S(2)}, u32[]{:S(2)}) collective-permute-start(f32[2,32,256]{2,1,0:T(8,128)S(1)} %add.142), channel_id=1, source_target_pairs={{0,192},{1,193},{2,194},{3,195},{8,200},{9,201},{10,202},{11,203},... | collective-permute-start | bytes 196616 | tf_op jit(solution)/shard_map/ppermute | solution.py:34
  80.1 9.2 %collective-permute-start.23 = (f32[2,32,256]{2,1,0:T(8,128)S(1)}, f32[2,32,256]{2,1,0:T(8,128)S(1)}, u32[]{:S(2)}, u32[]{:S(2)}) collective-permute-start(f32[2,32,256]{2,1,0:T(8,128)S(1)} %add_add_fusion.1), channel_id=1, source_target_pairs={{0,16},{1,17},{2,18},{3,19},{8,24},{9,25},{10,26},{11,27},{16,0},{... | collective-permute-start | bytes 196616 | tf_op jit(solution)/shard_map/ppermute | solution.py:34
  81.3 8.1 %collective-permute-start.24 = (f32[2,32,256]{2,1,0:T(8,128)S(1)}, f32[2,32,256]{2,1,0:T(8,128)S(1)}, u32[]{:S(2)}, u32[]{:S(2)}) collective-permute-start(f32[2,32,256]{2,1,0:T(8,128)S(1)} %add_add_fusion.1), channel_id=1, source_target_pairs={{0,32},{1,33},{2,34},{3,35},{8,40},{9,41},{10,42},{11,43},{16,48},... | collective-permute-start | bytes 196616 | tf_op jit(solution)/shard_map/ppermute | solution.py:34
  83.1 6.3 %collective-permute-start.25 = (f32[2,32,256]{2,1,0:T(8,128)S(1)}, f32[2,32,256]{2,1,0:T(8,128)S(1)}, u32[]{:S(2)}, u32[]{:S(2)}) collective-permute-start(f32[2,32,256]{2,1,0:T(8,128)S(1)} %add_add_fusion.1), channel_id=1, source_target_pairs={{0,48},{1,49},{2,50},{3,51},{8,56},{9,57},{10,58},{11,59},{16,32},... | collective-permute-start | bytes 196616 | tf_op jit(solution)/shard_map/ppermute | solution.py:34
  84.9 10.5 %collective-permute-start.15 = (bf16[4,128,128]{2,1,0:T(8,128)(2,1)S(1)}, bf16[4,128,128]{2,1,0:T(8,128)(2,1)S(1)}, u32[]{:S(2)}, u32[]{:S(2)}) collective-permute-start(bf16[4,128,128]{2,1,0:T(8,128)(2,1)S(1)} %add_convert_fusion.mine), channel_id=1, source_target_pairs={{0,4},{4,0},{1,5},{5,1},{2,6},{6,2},{3,7},{7,3},{8,12},{12,8},{9,1... | collective-permute-start | bytes 393224 | tf_op jit(solution)/shard_map/ppermute | solution.py:63
  95.7 6.3 %collective-permute-start.26 = (bf16[640,128]{1,0:T(8,128)(2,1)S(1)}, bf16[640,128]{1,0:T(8,128)(2,1)S(1)}, u32[]{:S(2)}, u32[]{:S(2)}) collective-permute-start(bf16[640,128]{1,0:T(8,128)(2,1)S(1)} %finish.1), channel_id=1, source_target_pairs={{0,3},{1,0},{2,1},{3,2},{4,7},{5,4},{6,5},{7,6},{8,11},{9,8},{10,9... | collective-permute-start | bytes 491528 | tf_op jit(solution)/shard_map/ppermute | solution.py:59
  96.8 6.9 %collective-permute-start.27 = (bf16[640,128]{1,0:T(8,128)(2,1)S(1)}, bf16[640,128]{1,0:T(8,128)(2,1)S(1)}, u32[]{:S(2)}, u32[]{:S(2)}) collective-permute-start(bf16[640,128]{1,0:T(8,128)(2,1)S(1)} %finish.1), channel_id=1, source_target_pairs={{0,2},{1,3},{2,0},{3,1},{4,6},{5,7},{6,4},{7,5},{8,10},{9,11},{10,... | collective-permute-start | bytes 491528 | tf_op jit(solution)/shard_map/ppermute | solution.py:59
  98.3 7.7 %collective-permute-start.28 = (bf16[640,128]{1,0:T(8,128)(2,1)S(1)}, bf16[640,128]{1,0:T(8,128)(2,1)S(1)}, u32[]{:S(2)}, u32[]{:S(2)}) collective-permute-start(bf16[640,128]{1,0:T(8,128)(2,1)S(1)} %finish.1), channel_id=1, source_target_pairs={{0,1},{1,2},{2,3},{3,0},{4,5},{5,6},{6,7},{7,4},{8,9},{9,10},{10,1... | collective-permute-start | bytes 491528 | tf_op jit(solution)/shard_map/ppermute | solution.py:59

commit v3 on v2

--- a/solution.py
+++ b/solution.py
@@ -281,8 +281,6 @@
     step3 = send(near, along(3))
     far = send(near, lambda z, y, core, r: (z, y, core, r - 1 if core == 0 else r + 1))
     step2 = send(step1, along(1))
-    near_x, step1_x, step3_x, far_x = (send(x, to_core) for x in (near, step1, step3, far))
-    pairs = [(near, far_x), (step1, step3_x), (step3, step1_x), (far, near_x)]
     items = lambda plan: [i for i, _, _ in plan]
     g_other = send_col(g_own)
     g_other = after(g_other, step1, step3, far)
@@ -303,8 +301,12 @@
     )
     rows_each = partial.shape[1] // NR
     for_rep = lambda s: lax.dynamic_slice_in_dim(partial, (rep + s) % NR * rows_each, rows_each, 1)
-    step2, *parts = lax.optimization_barrier((step2, *(for_rep(s) for s in range(NR))))
-    step2_x = send(step2, to_core)
+    parts = [for_rep(s) for s in range(NR)]
+    step1, step3, far, *parts = lax.optimization_barrier((step1, step3, far, *parts))
+    near_x, step1_x, step3_x, far_x, step2_x = (
+        send(x, to_core) for x in (near, step1, step3, far, step2)
+    )
+    pairs = [(near, far_x), (step1, step3_x), (step3, step1_x), (far, near_x)]
     acc = spmm(table, 1, tv, items(outer), pairs)
     got = [send_rep(parts[s], s) for s in range(1, NR)]
     piece = parts[0] + sum(lax.optimization_barrier((*got, acc))[:-1])
@@ -314,8 +316,8 @@
     total = own + sum(send_rep(x, s).astype(F32) for s, x in enumerate(outs, 1))
     mine = total.astype(BF)
     theirs = send_col(mine)
-    piece = sum_four(after(piece, own), "z", mine)
-    piece = sum_four(piece, "y", theirs).reshape(TILE, TILE)
+    piece = sum_four(after(piece, own), "y", mine)
+    piece = sum_four(after(piece, theirs), "z", theirs).reshape(TILE, TILE)
     scale = 1.0 / math.sqrt(row_count * lax.axis_size("blk"))
     block = finish(mine, theirs, wn, self_term, piece, scale)
     blocks = [block] + [send_rep(block, s) for s in range(1, NR)]

time: 109 us -> 111 us (1.018)
  starting transfers between devices: 49.5 us -> 52.6 us
  waiting for transfers between devices: 39.5 us -> 38 us
    ppermute x2, starting transfers between devices: 6.78 us -> 11 us  [send_col(): return lax.ppermute(x, 'col', [(0, 1), (1, 0)])]
    ppermute x9, waiting for transfers between devices: 6.56 us -> 10.1 us  [send_rep(): return lax.ppermute(x, 'rep', [(r, (r + s) % NR) for r in range(NR)])]
    ppermute x2, waiting for transfers between devices: 12 us -> 9.33 us  [send_col(): return lax.ppermute(x, 'col', [(0, 1), (1, 0)])]
    ppermute x18, waiting for transfers between devices: 20.9 us -> 18.6 us  [send(): return lax.ppermute(x, ('blk', 'rep'), route)]
    ppermute x9, starting transfers between devices: 14.5 us -> 12.8 us  [send_rep(): return lax.ppermute(x, 'rep', [(r, (r + s) % NR) for r in range(NR)])]
  transfers between devices with their start and end apart: 29 -> 29, of which waited for: 13 -> 13; matrix products, arithmetic and copies ran while one was open for 5% -> 5% of each run, Pallas kernels for 5% -> 6%
where the time goes in v3:
time: 111 us; the launch traced here: 110 us
  starting transfers between devices  52.6 us (47%)
  waiting for transfers between devices  38 us (34%)
  Pallas kernels  11 us (10%)
  other arithmetic  3.69 us (3%)
  local copies, waits for them, and re-layouts  2.11 us (2%)
  matrix products  1.59 us (1%)
    ppermute x18, starting transfers between devices, send(): return lax.ppermute(x, ('blk', 'rep'), route)  28.8 us
    ppermute x18, waiting for transfers between devices, send(): return lax.ppermute(x, ('blk', 'rep'), route)  18.6 us
    ppermute x9, starting transfers between devices, send_rep(): return lax.ppermute(x, 'rep', [(r, (r + s) % NR) for r in range(NR)])  12.8 us
    ppermute x2, starting transfers between devices, send_col(): return lax.ppermute(x, 'col', [(0, 1), (1, 0)])  11 us
    ppermute x9, waiting for transfers between devices, send_rep(): return lax.ppermute(x, 'rep', [(r, (r + s) % NR) for r in range(NR)])  10.1 us
    ppermute x2, waiting for transfers between devices, send_col(): return lax.ppermute(x, 'col', [(0, 1), (1, 0)])  9.33 us
    pallas_call x2, Pallas kernels, spmm(): pl.pallas_call(functools.partial(spmm_kernel, items, last, base), out_sha...  8.76 us
  transfers between devices with their start and end apart: 29, of which 13 were waited for; matrix products, arithmetic and copies ran while one was open for 5% of the time, Pallas kernels for 6%

profile of v3, /device:TPU:32, one launch (start us, length us, event | category | flops | bytes accessed | tf_op | source)
XLA Modules:
  0.0 110.0 jit_solution(16516473224973767346)
XLA Ops:
  0.7 2.0 %prep.1 = (bf16[16,64,128]{2,1,0:T(8,128)(2,1)S(1)}, bf16[16,64,128]{2,1,0:T(8,128)(2,1)S(1)}) custom-call(s32[2]{0:T(128)S(1)} %pad_add_fusion.1.ids, bf16[16,128,128]{2,1,0:T(8,128)(2,1)} %bitcast.65, s32[16,128]{1,0:T(8,128)} %bitcast.67), custom_call_target="tpu_custom_call" | custom-call | flops 1048576 | bytes 1048576 | tf_op jit(solution)/shard_map/prep/pallas_call | solution.py:107
  4.4 2.9 %collective-permute-start.1 = (bf16[2,16,64,128]{3,2,1,0:T(8,128)(2,1)S(1)}, bf16[2,16,64,128]{3,2,1,0:T(8,128)(2,1)S(1)}, u32[]{:S(2)}, u32[]{:S(2)}) collective-permute-start(bf16[2,16,64,128]{3,2,1,0:T(8,128)(2,1)S(1)} %pad_maximum_fusion), channel_id=1, source_target_pairs={{0,65},{1,0},{2,130},{3,195},{8,72},{9,137},{10,11},{11,202},{16,8... | collective-permute-start | bytes 1572872 | tf_op jit(solution)/shard_map/ppermute | solution.py:34
  10.1 7.8 %collective-permute-done.1.refs_0_ = bf16[2,16,64,128]{3,2,1,0:T(8,128)(2,1)S(1)} collective-permute-done((bf16[2,16,64,128]{3,2,1,0:T(8,128)(2,1)S(1)}, bf16[2,16,64,128]{3,2,1,0:T(8,128)(2,1)S(1)}, u32[]{:S(2)}, u32[]{:S(2)}) %collective-permute-start.1) | collective-permute-done | bytes 524320 | tf_op jit(solution)/shard_map/ppermute | solution.py:34
  17.9 1.6 %collective-permute-start.2 = (bf16[2,16,64,128]{3,2,1,0:T(8,128)(2,1)S(1)}, bf16[2,16,64,128]{3,2,1,0:T(8,128)(2,1)S(1)}, u32[]{:S(2)}, u32[]{:S(2)}) collective-permute-start(bf16[2,16,64,128]{3,2,1,0:T(8,128)(2,1)S(1)} %collective-permute-done.1.refs_0_), channel_id=1, source_target_pairs={{0,16},{1,17},{2,18},{3,19},{8,57},{9,58},{10,59},{11,56},{16,32},... | collective-permute-start | bytes 1572872 | tf_op jit(solution)/shard_map/ppermute | solution.py:34
  19.5 4.7 %collective-permute-start.5 = (bf16[2,16,64,128]{3,2,1,0:T(8,128)(2,1)S(1)}, bf16[2,16,64,128]{3,2,1,0:T(8,128)(2,1)S(1)}, u32[]{:S(2)}, u32[]{:S(2)}) collective-permute-start(bf16[2,16,64,128]{3,2,1,0:T(8,128)(2,1)S(1)} %collective-permute-done.1.refs_0_), channel_id=1, source_target_pairs={{0,48},{1,49},{2,50},{3,51},{8,25},{9,26},{10,27},{11,24},{16,3},{... | collective-permute-start | bytes 1572872 | tf_op jit(solution)/shard_map/ppermute | solution.py:34
  24.1 1.7 %collective-permute-start.6 = (bf16[2,16,64,128]{3,2,1,0:T(8,128)(2,1)S(1)}, bf16[2,16,64,128]{3,2,1,0:T(8,128)(2,1)S(1)}, u32[]{:S(2)}, u32[]{:S(2)}) collective-permute-start(bf16[2,16,64,128]{3,2,1,0:T(8,128)(2,1)S(1)} %collective-permute-done.1.refs_0_), channel_id=1, source_target_pairs={{0,3},{1,0},{2,1},{3,2},{8,9},{9,10},{10,11},{11,8},{16,19},{17,16... | collective-permute-start | bytes 1572872 | tf_op jit(solution)/shard_map/ppermute | solution.py:34
  25.9 3.7 %collective-permute-done.2.refs_2_ = bf16[2,16,64,128]{3,2,1,0:T(8,128)(2,1)S(1)} collective-permute-done((bf16[2,16,64,128]{3,2,1,0:T(8,128)(2,1)S(1)}, bf16[2,16,64,128]{3,2,1,0:T(8,128)(2,1)S(1)}, u32[]{:S(2)}, u32[]{:S(2)}) %collective-permute-start.2) | collective-permute-done | bytes 524320 | tf_op jit(solution)/shard_map/ppermute | solution.py:34
  29.6 3.6 %collective-permute-start.3 = (bf16[2,16,64,128]{3,2,1,0:T(8,128)(2,1)S(1)}, bf16[2,16,64,128]{3,2,1,0:T(8,128)(2,1)S(1)}, u32[]{:S(2)}, u32[]{:S(2)}) collective-permute-start(bf16[2,16,64,128]{3,2,1,0:T(8,128)(2,1)S(1)} %collective-permute-done.2.refs_2_), channel_id=1, source_target_pairs={{0,16},{1,17},{2,18},{3,19},{8,57},{9,58},{10,59},{11,56},{16,32},... | collective-permute-start | bytes 1572872 | tf_op jit(solution)/shard_map/ppermute | solution.py:34
  33.2 5.5 %collective-permute-start.7 = (bf16[512,128]{1,0:T(8,128)(2,1)S(1)}, bf16[512,128]{1,0:T(8,128)(2,1)S(1)}, u32[]{:S(2)}, u32[]{:S(2)}) collective-permute-start(bf16[512,128]{1,0:T(8,128)(2,1)S(1)} %constant_dynamic-slice_fusion), channel_id=1, source_target_pairs={{0,4},{4,0},{1,5},{5,1},{2,6},{6,2},{3,7},{7,3},{8,12},{12,8},{9,1... | collective-permute-start | bytes 393224 | tf_op jit(solution)/shard_map/ppermute | solution.py:63
  38.7 5.5 %collective-permute-done.7 = bf16[512,128]{1,0:T(8,128)(2,1)S(1)} collective-permute-done((bf16[512,128]{1,0:T(8,128)(2,1)S(1)}, bf16[512,128]{1,0:T(8,128)(2,1)S(1)}, u32[]{:S(2)}, u32[]{:S(2)}) %collective-permute-start.7) | collective-permute-done | bytes 131104 | tf_op jit(solution)/shard_map/ppermute | solution.py:63
  44.5 1.1 %convolution_bitcast_fusion.1 = f32[1,128,256]{2,1,0:T(8,128)S(1)} fusion(bf16[2048,128]{1,0:T(8,128)(2,1)} %param.10, s32[]{:T(128)S(6)} %select_n.155, bf16[512,128]{1,0:T(8,128)(2,1)S(1)} %collective-permute-done.7, bf16[512,128]{1,0:T(8,128)(2,1)S(1)} %constant_dynamic-slice_fusion, pred[]{:T(512)S(6)} %eq.13), kind=kOutput, calls=%fused_computation.1 | convolution fusion | flops 34734080 | bytes 524293 | tf_op jit(solution)/shard_map/dot_general | solution.py:298
  46.8 2.3 %collective-permute-start.16 = (f32[2,32,256]{2,1,0:T(8,128)S(1)}, f32[2,32,256]{2,1,0:T(8,128)S(1)}, u32[]{:S(2)}, u32[]{:S(2)}) collective-permute-start(f32[2,32,256]{2,1,0:T(8,128)S(1)} %get-tuple-element.50), channel_id=1, source_target_pairs={{0,1},{1,2},{2,3},{3,0},{4,5},{5,6},{6,7},{7,4},{8,9},{9,10},{10,1... | collective-permute-start | bytes 196616 | tf_op jit(solution)/shard_map/ppermute | solution.py:59
  49.1 3.3 %collective-permute-start.17 = (f32[2,32,256]{2,1,0:T(8,128)S(1)}, f32[2,32,256]{2,1,0:T(8,128)S(1)}, u32[]{:S(2)}, u32[]{:S(2)}) collective-permute-start(f32[2,32,256]{2,1,0:T(8,128)S(1)} %get-tuple-element.51), channel_id=1, source_target_pairs={{0,2},{1,3},{2,0},{3,1},{4,6},{5,7},{6,4},{7,5},{8,10},{9,11},{10,... | collective-permute-start | bytes 196616 | tf_op jit(solution)/shard_map/ppermute | solution.py:59
  52.4 1.1 %collective-permute-start.18 = (f32[2,32,256]{2,1,0:T(8,128)S(1)}, f32[2,32,256]{2,1,0:T(8,128)S(1)}, u32[]{:S(2)}, u32[]{:S(2)}) collective-permute-start(f32[2,32,256]{2,1,0:T(8,128)S(1)} %get-tuple-element.52), channel_id=1, source_target_pairs={{0,3},{1,0},{2,1},{3,2},{4,7},{5,4},{6,5},{7,6},{8,11},{9,8},{10,9... | collective-permute-start | bytes 196616 | tf_op jit(solution)/shard_map/ppermute | solution.py:59
  53.5 6.2 %tiles.2.refs_2_ = f32[16,128,128]{2,1,0:T(8,128)S(1)} custom-call(s32[9,81]{1,0:T(8,128)S(1)} %pad_add_fusion.table, bf16[1,8,40,128,128]{4,3,2,1,0:T(8,128)(2,1)} %tv.3, bf16[2,16,64,128]{3,2,1,0:T(8,128)(2,1)S(1)} %collective-permute-done.1.refs_0_, bf16[2,16,64,128]{3,2,1,0:T(8,128)(2,1)S(1)} %collective-permute-done.8.refs_1_, ...), custom_call_target="tpu_custom_call" | custom-call | flops 293601280 | bytes 7340032 | tf_op jit(solution)/shard_map/tiles/pallas_call | solution.py:190
  59.8 2.6 %tiles.3 = (f32[4,128,128]{2,1,0:T(8,128)S(1)}, bf16[4,128,128]{2,1,0:T(8,128)(2,1)S(1)}, bf16[4,128,128]{2,1,0:T(8,128)(2,1)S(1)}, bf16[4,128,128]{2,1,0:T(8,128)(2,1)S(1)}) custom-call(s32[9,81]{1,0:T(8,128)S(1)} %pad_add_fusion.table, bf16[1,8,40,128,128]{4,3,2,1,0:T(8,128)(2,1)} %tv.3, bf16[2,16,64,128]{3,2,1,0:T(8,128)(2,1)S(1)} %collective-permute-done.3.refs_0_, ...), custom_call_target="tpu_custom_call" | custom-call | flops 83886080 | bytes 2097152 | tf_op jit(solution)/shard_map/tiles/pallas_call | solution.py:190
  63.3 3.0 %collective-permute-start.13 = (bf16[4,128,128]{2,1,0:T(8,128)(2,1)S(1)}, bf16[4,128,128]{2,1,0:T(8,128)(2,1)S(1)}, u32[]{:S(2)}, u32[]{:S(2)}) collective-permute-start(bf16[4,128,128]{2,1,0:T(8,128)(2,1)S(1)} %get-tuple-element.46), channel_id=1, source_target_pairs={{0,2},{1,3},{2,0},{3,1},{4,6},{5,7},{6,4},{7,5},{8,10},{9,11},{10,... | collective-permute-start | bytes 393224 | tf_op jit(solution)/shard_map/ppermute | solution.py:59
  66.4 1.2 %collective-permute-done.19 = f32[2,32,256]{2,1,0:T(8,128)S(1)} collective-permute-done((f32[2,32,256]{2,1,0:T(8,128)S(1)}, f32[2,32,256]{2,1,0:T(8,128)S(1)}, u32[]{:S(2)}, u32[]{:S(2)}) %collective-permute-start.19) | collective-permute-done | bytes 65568 | tf_op jit(solution)/shard_map/ppermute | solution.py:34
  67.7 1.4 %collective-permute-start.20 = (f32[2,32,256]{2,1,0:T(8,128)S(1)}, f32[2,32,256]{2,1,0:T(8,128)S(1)}, u32[]{:S(2)}, u32[]{:S(2)}) collective-permute-start(f32[2,32,256]{2,1,0:T(8,128)S(1)} %add.142), channel_id=1, source_target_pairs={{0,16},{1,17},{2,18},{3,19},{8,24},{9,25},{10,26},{11,27},{16,0},{... | collective-permute-start | bytes 196616 | tf_op jit(solution)/shard_map/ppermute | solution.py:34
  69.0 1.9 %collective-permute-start.21 = (f32[2,32,256]{2,1,0:T(8,128)S(1)}, f32[2,32,256]{2,1,0:T(8,128)S(1)}, u32[]{:S(2)}, u32[]{:S(2)}) collective-permute-start(f32[2,32,256]{2,1,0:T(8,128)S(1)} %add.142), channel_id=1, source_target_pairs={{0,32},{1,33},{2,34},{3,35},{8,40},{9,41},{10,42},{11,43},{16,48},... | collective-permute-start | bytes 196616 | tf_op jit(solution)/shard_map/ppermute | solution.py:34
  70.9 1.9 %collective-permute-done.12 = bf16[4,128,128]{2,1,0:T(8,128)(2,1)S(1)} collective-permute-done((bf16[4,128,128]{2,1,0:T(8,128)(2,1)S(1)}, bf16[4,128,128]{2,1,0:T(8,128)(2,1)S(1)}, u32[]{:S(2)}, u32[]{:S(2)}) %collective-permute-start.12) | collective-permute-done | bytes 131104 | tf_op jit(solution)/shard_map/ppermute | solution.py:59
  72.8 1.2 %collective-permute-start.22 = (f32[2,32,256]{2,1,0:T(8,128)S(1)}, f32[2,32,256]{2,1,0:T(8,128)S(1)}, u32[]{:S(2)}, u32[]{:S(2)}) collective-permute-start(f32[2,32,256]{2,1,0:T(8,128)S(1)} %add.142), channel_id=1, source_target_pairs={{0,48},{1,49},{2,50},{3,51},{8,56},{9,57},{10,58},{11,59},{16,32},... | collective-permute-start | bytes 196616 | tf_op jit(solution)/shard_map/ppermute | solution.py:34
  74.0 5.5 %collective-permute-start.15 = (bf16[4,128,128]{2,1,0:T(8,128)(2,1)S(1)}, bf16[4,128,128]{2,1,0:T(8,128)(2,1)S(1)}, u32[]{:S(2)}, u32[]{:S(2)}) collective-permute-start(bf16[4,128,128]{2,1,0:T(8,128)(2,1)S(1)} %add_convert_fusion.mine), channel_id=1, source_target_pairs={{0,4},{4,0},{1,5},{5,1},{2,6},{6,2},{3,7},{7,3},{8,12},{12,8},{9,1... | collective-permute-start | bytes 393224 | tf_op jit(solution)/shard_map/ppermute | solution.py:63
  79.6 3.9 %collective-permute-done.15.theirs = bf16[4,128,128]{2,1,0:T(8,128)(2,1)S(1)} collective-permute-done((bf16[4,128,128]{2,1,0:T(8,128)(2,1)S(1)}, bf16[4,128,128]{2,1,0:T(8,128)(2,1)S(1)}, u32[]{:S(2)}, u32[]{:S(2)}) %collective-permute-start.15) | collective-permute-done | bytes 131104 | tf_op jit(solution)/shard_map/ppermute | solution.py:63
  83.4 2.0 %collective-permute-start.23 = (f32[2,32,256]{2,1,0:T(8,128)S(1)}, f32[2,32,256]{2,1,0:T(8,128)S(1)}, u32[]{:S(2)}, u32[]{:S(2)}) collective-permute-start(f32[2,32,256]{2,1,0:T(8,128)S(1)} %add_add_fusion.1), channel_id=1, source_target_pairs={{0,64},{1,65},{2,66},{3,67},{8,72},{9,73},{10,74},{11,75},{16,80},... | collective-permute-start | bytes 196616 | tf_op jit(solution)/shard_map/ppermute | solution.py:34
  85.4 6.1 %collective-permute-start.24 = (f32[2,32,256]{2,1,0:T(8,128)S(1)}, f32[2,32,256]{2,1,0:T(8,128)S(1)}, u32[]{:S(2)}, u32[]{:S(2)}) collective-permute-start(f32[2,32,256]{2,1,0:T(8,128)S(1)} %add_add_fusion.1), channel_id=1, source_target_pairs={{0,128},{1,129},{2,130},{3,131},{8,136},{9,137},{10,138},{11,139},... | collective-permute-start | bytes 196616 | tf_op jit(solution)/shard_map/ppermute | solution.py:34
  92.4 3.9 %collective-permute-done.24 = f32[2,32,256]{2,1,0:T(8,128)S(1)} collective-permute-done((f32[2,32,256]{2,1,0:T(8,128)S(1)}, f32[2,32,256]{2,1,0:T(8,128)S(1)}, u32[]{:S(2)}, u32[]{:S(2)}) %collective-permute-start.24) | collective-permute-done | bytes 65568 | tf_op jit(solution)/shard_map/ppermute | solution.py:34
  96.3 1.0 collective-permute-done.25
  98.1 1.7 %collective-permute-start.28 = (bf16[640,128]{1,0:T(8,128)(2,1)S(1)}, bf16[640,128]{1,0:T(8,128)(2,1)S(1)}, u32[]{:S(2)}, u32[]{:S(2)}) collective-permute-start(bf16[640,128]{1,0:T(8,128)(2,1)S(1)} %finish.1), channel_id=1, source_target_pairs={{0,1},{1,2},{2,3},{3,0},{4,5},{5,6},{6,7},{7,4},{8,9},{9,10},{10,1... | collective-permute-start | bytes 491528 | tf_op jit(solution)/shard_map/ppermute | solution.py:59
  99.8 4.9 %collective-permute-done.26 = bf16[640,128]{1,0:T(8,128)(2,1)S(1)} collective-permute-done((bf16[640,128]{1,0:T(8,128)(2,1)S(1)}, bf16[640,128]{1,0:T(8,128)(2,1)S(1)}, u32[]{:S(2)}, u32[]{:S(2)}) %collective-permute-start.26) | collective-permute-done | bytes 163872 | tf_op jit(solution)/shard_map/ppermute | solution.py:59
  104.7 1.6 %collective-permute-done.27 = bf16[640,128]{1,0:T(8,128)(2,1)S(1)} collective-permute-done((bf16[640,128]{1,0:T(8,128)(2,1)S(1)}, bf16[640,128]{1,0:T(8,128)(2,1)S(1)}, u32[]{:S(2)}, u32[]{:S(2)}) %collective-permute-start.27) | collective-permute-done | bytes 163872 | tf_op jit(solution)/shard_map/ppermute | solution.py:59
  106.4 1.7 %collective-permute-done.28 = bf16[640,128]{1,0:T(8,128)(2,1)S(1)} collective-permute-done((bf16[640,128]{1,0:T(8,128)(2,1)S(1)}, bf16[640,128]{1,0:T(8,128)(2,1)S(1)}, u32[]{:S(2)}, u32[]{:S(2)}) %collective-permute-start.28) | collective-permute-done | bytes 163872 | tf_op jit(solution)/shard_map/ppermute | solution.py:59
  (82 shorter events, 10.6 us)
Async XLA Ops:
  0.6 43.6 %copy-start = (bf16[2048,128]{1,0:T(8,128)(2,1)S(1)}, bf16[2048,128]{1,0:T(8,128)(2,1)}, u32[]{:S(2)}) copy-start(bf16[2048,128]{1,0:T(8,128)(2,1)} %param.11) | copy-start | bytes 1572868
  2.7 1.6 %collective-permute-start = (bf16[16,64,128]{2,1,0:T(8,128)(2,1)S(1)}, bf16[16,64,128]{2,1,0:T(8,128)(2,1)S(1)}, u32[]{:S(2)}, u32[]{:S(2)}) collective-permute-start(bf16[16,64,128]{2,1,0:T(8,128)(2,1)S(1)} %get-tuple-element.34), channel_id=1, source_target_pairs={{0,8},{1,9},{2,10},{3,11},{8,0},{9,1},{10,2},{11,3},{16,24},{17,25... | collective-permute-start | bytes 786440 | tf_op jit(solution)/shard_map/ppermute | solution.py:34
  4.4 13.5 %collective-permute-start.1 = (bf16[2,16,64,128]{3,2,1,0:T(8,128)(2,1)S(1)}, bf16[2,16,64,128]{3,2,1,0:T(8,128)(2,1)S(1)}, u32[]{:S(2)}, u32[]{:S(2)}) collective-permute-start(bf16[2,16,64,128]{3,2,1,0:T(8,128)(2,1)S(1)} %pad_maximum_fusion), channel_id=1, source_target_pairs={{0,65},{1,0},{2,130},{3,195},{8,72},{9,137},{10,11},{11,202},{16,8... | collective-permute-start | bytes 1572872 | tf_op jit(solution)/shard_map/ppermute | solution.py:34
  17.9 11.7 %collective-permute-start.2 = (bf16[2,16,64,128]{3,2,1,0:T(8,128)(2,1)S(1)}, bf16[2,16,64,128]{3,2,1,0:T(8,128)(2,1)S(1)}, u32[]{:S(2)}, u32[]{:S(2)}) collective-permute-start(bf16[2,16,64,128]{3,2,1,0:T(8,128)(2,1)S(1)} %collective-permute-done.1.refs_0_), channel_id=1, source_target_pairs={{0,16},{1,17},{2,18},{3,19},{8,57},{9,58},{10,59},{11,56},{16,32},... | collective-permute-start | bytes 1572872 | tf_op jit(solution)/shard_map/ppermute | solution.py:34
  19.5 24.8 %collective-permute-start.5 = (bf16[2,16,64,128]{3,2,1,0:T(8,128)(2,1)S(1)}, bf16[2,16,64,128]{3,2,1,0:T(8,128)(2,1)S(1)}, u32[]{:S(2)}, u32[]{:S(2)}) collective-permute-start(bf16[2,16,64,128]{3,2,1,0:T(8,128)(2,1)S(1)} %collective-permute-done.1.refs_0_), channel_id=1, source_target_pairs={{0,48},{1,49},{2,50},{3,51},{8,25},{9,26},{10,27},{11,24},{16,3},{... | collective-permute-start | bytes 1572872 | tf_op jit(solution)/shard_map/ppermute | solution.py:34
  24.1 20.1 %collective-permute-start.6 = (bf16[2,16,64,128]{3,2,1,0:T(8,128)(2,1)S(1)}, bf16[2,16,64,128]{3,2,1,0:T(8,128)(2,1)S(1)}, u32[]{:S(2)}, u32[]{:S(2)}) collective-permute-start(bf16[2,16,64,128]{3,2,1,0:T(8,128)(2,1)S(1)} %collective-permute-done.1.refs_0_), channel_id=1, source_target_pairs={{0,3},{1,0},{2,1},{3,2},{8,9},{9,10},{10,11},{11,8},{16,19},{17,16... | collective-permute-start | bytes 1572872 | tf_op jit(solution)/shard_map/ppermute | solution.py:34
  29.6 16.8 %collective-permute-start.3 = (bf16[2,16,64,128]{3,2,1,0:T(8,128)(2,1)S(1)}, bf16[2,16,64,128]{3,2,1,0:T(8,128)(2,1)S(1)}, u32[]{:S(2)}, u32[]{:S(2)}) collective-permute-start(bf16[2,16,64,128]{3,2,1,0:T(8,128)(2,1)S(1)} %collective-permute-done.2.refs_2_), channel_id=1, source_target_pairs={{0,16},{1,17},{2,18},{3,19},{8,57},{9,58},{10,59},{11,56},{16,32},... | collective-permute-start | bytes 1572872 | tf_op jit(solution)/shard_map/ppermute | solution.py:34
  33.2 11.0 %collective-permute-start.7 = (bf16[512,128]{1,0:T(8,128)(2,1)S(1)}, bf16[512,128]{1,0:T(8,128)(2,1)S(1)}, u32[]{:S(2)}, u32[]{:S(2)}) collective-permute-start(bf16[512,128]{1,0:T(8,128)(2,1)S(1)} %constant_dynamic-slice_fusion), channel_id=1, source_target_pairs={{0,4},{4,0},{1,5},{5,1},{2,6},{6,2},{3,7},{7,3},{8,12},{12,8},{9,1... | collective-permute-start | bytes 393224 | tf_op jit(solution)/shard_map/ppermute | solution.py:63
  38.7 8.0 %collective-permute-start.11 = (bf16[2,16,64,128]{3,2,1,0:T(8,128)(2,1)S(1)}, bf16[2,16,64,128]{3,2,1,0:T(8,128)(2,1)S(1)}, u32[]{:S(2)}, u32[]{:S(2)}) collective-permute-start(bf16[2,16,64,128]{3,2,1,0:T(8,128)(2,1)S(1)} %collective-permute-done.1.refs_0_), channel_id=1, source_target_pairs={{0,8},{1,9},{2,10},{3,11},{8,0},{9,1},{10,2},{11,3},{16,24},{17,25... | collective-permute-start | bytes 1572872 | tf_op jit(solution)/shard_map/ppermute | solution.py:34
  45.6 3.5 %collective-permute-start.10 = (bf16[2,16,64,128]{3,2,1,0:T(8,128)(2,1)S(1)}, bf16[2,16,64,128]{3,2,1,0:T(8,128)(2,1)S(1)}, u32[]{:S(2)}, u32[]{:S(2)}) collective-permute-start(bf16[2,16,64,128]{3,2,1,0:T(8,128)(2,1)S(1)} %collective-permute-done.2.refs_2_), channel_id=1, source_target_pairs={{0,8},{1,9},{2,10},{3,11},{8,0},{9,1},{10,2},{11,3},{16,24},{17,25... | collective-permute-start | bytes 1572872 | tf_op jit(solution)/shard_map/ppermute | solution.py:34
  45.7 6.6 %collective-permute-start.8 = (bf16[2,16,64,128]{3,2,1,0:T(8,128)(2,1)S(1)}, bf16[2,16,64,128]{3,2,1,0:T(8,128)(2,1)S(1)}, u32[]{:S(2)}, u32[]{:S(2)}) collective-permute-start(bf16[2,16,64,128]{3,2,1,0:T(8,128)(2,1)S(1)} %collective-permute-done.6.refs_6_), channel_id=1, source_target_pairs={{0,8},{1,9},{2,10},{3,11},{8,0},{9,1},{10,2},{11,3},{16,24},{17,25... | collective-permute-start | bytes 1572872 | tf_op jit(solution)/shard_map/ppermute | solution.py:34
  46.2 7.2 %collective-permute-start.9 = (bf16[2,16,64,128]{3,2,1,0:T(8,128)(2,1)S(1)}, bf16[2,16,64,128]{3,2,1,0:T(8,128)(2,1)S(1)}, u32[]{:S(2)}, u32[]{:S(2)}) collective-permute-start(bf16[2,16,64,128]{3,2,1,0:T(8,128)(2,1)S(1)} %collective-permute-done.5.refs_4_), channel_id=1, source_target_pairs={{0,8},{1,9},{2,10},{3,11},{8,0},{9,1},{10,2},{11,3},{16,24},{17,25... | collective-permute-start | bytes 1572872 | tf_op jit(solution)/shard_map/ppermute | solution.py:34
  46.4 13.3 %collective-permute-start.4 = (bf16[2,16,64,128]{3,2,1,0:T(8,128)(2,1)S(1)}, bf16[2,16,64,128]{3,2,1,0:T(8,128)(2,1)S(1)}, u32[]{:S(2)}, u32[]{:S(2)}) collective-permute-start(bf16[2,16,64,128]{3,2,1,0:T(8,128)(2,1)S(1)} %collective-permute-done.3.refs_0_), channel_id=1, source_target_pairs={{0,8},{1,9},{2,10},{3,11},{8,0},{9,1},{10,2},{11,3},{16,24},{17,25... | collective-permute-start | bytes 1572872 | tf_op jit(solution)/shard_map/ppermute | solution.py:34
  46.8 13.0 %collective-permute-start.16 = (f32[2,32,256]{2,1,0:T(8,128)S(1)}, f32[2,32,256]{2,1,0:T(8,128)S(1)}, u32[]{:S(2)}, u32[]{:S(2)}) collective-permute-start(f32[2,32,256]{2,1,0:T(8,128)S(1)} %get-tuple-element.50), channel_id=1, source_target_pairs={{0,1},{1,2},{2,3},{3,0},{4,5},{5,6},{6,7},{7,4},{8,9},{9,10},{10,1... | collective-permute-start | bytes 196616 | tf_op jit(solution)/shard_map/ppermute | solution.py:59
  49.1 10.6 %collective-permute-start.17 = (f32[2,32,256]{2,1,0:T(8,128)S(1)}, f32[2,32,256]{2,1,0:T(8,128)S(1)}, u32[]{:S(2)}, u32[]{:S(2)}) collective-permute-start(f32[2,32,256]{2,1,0:T(8,128)S(1)} %get-tuple-element.51), channel_id=1, source_target_pairs={{0,2},{1,3},{2,0},{3,1},{4,6},{5,7},{6,4},{7,5},{8,10},{9,11},{10,... | collective-permute-start | bytes 196616 | tf_op jit(solution)/shard_map/ppermute | solution.py:59
  52.4 7.4 %collective-permute-start.18 = (f32[2,32,256]{2,1,0:T(8,128)S(1)}, f32[2,32,256]{2,1,0:T(8,128)S(1)}, u32[]{:S(2)}, u32[]{:S(2)}) collective-permute-start(f32[2,32,256]{2,1,0:T(8,128)S(1)} %get-tuple-element.52), channel_id=1, source_target_pairs={{0,3},{1,0},{2,1},{3,2},{4,7},{5,4},{6,5},{7,6},{8,11},{9,8},{10,9... | collective-permute-start | bytes 196616 | tf_op jit(solution)/shard_map/ppermute | solution.py:59
  59.7 32.4 %copy-start.1 = (bf16[128,256]{1,0:T(8,128)(2,1)S(1)}, bf16[128,256]{1,0:T(8,128)(2,1)}, u32[]{:S(2)}) copy-start(bf16[128,256]{1,0:T(8,128)(2,1)} %param.13) | copy-start | bytes 196612
  62.3 10.5 %collective-permute-start.12 = (bf16[4,128,128]{2,1,0:T(8,128)(2,1)S(1)}, bf16[4,128,128]{2,1,0:T(8,128)(2,1)S(1)}, u32[]{:S(2)}, u32[]{:S(2)}) collective-permute-start(bf16[4,128,128]{2,1,0:T(8,128)(2,1)S(1)} %get-tuple-element.45), channel_id=1, source_target_pairs={{0,1},{1,2},{2,3},{3,0},{4,5},{5,6},{6,7},{7,4},{8,9},{9,10},{10,1... | collective-permute-start | bytes 393224 | tf_op jit(solution)/shard_map/ppermute | solution.py:59
  63.3 10.6 %collective-permute-start.13 = (bf16[4,128,128]{2,1,0:T(8,128)(2,1)S(1)}, bf16[4,128,128]{2,1,0:T(8,128)(2,1)S(1)}, u32[]{:S(2)}, u32[]{:S(2)}) collective-permute-start(bf16[4,128,128]{2,1,0:T(8,128)(2,1)S(1)} %get-tuple-element.46), channel_id=1, source_target_pairs={{0,2},{1,3},{2,0},{3,1},{4,6},{5,7},{6,4},{7,5},{8,10},{9,11},{10,... | collective-permute-start | bytes 393224 | tf_op jit(solution)/shard_map/ppermute | solution.py:59
  66.3 7.7 %collective-permute-start.14 = (bf16[4,128,128]{2,1,0:T(8,128)(2,1)S(1)}, bf16[4,128,128]{2,1,0:T(8,128)(2,1)S(1)}, u32[]{:S(2)}, u32[]{:S(2)}) collective-permute-start(bf16[4,128,128]{2,1,0:T(8,128)(2,1)S(1)} %get-tuple-element.47), channel_id=1, source_target_pairs={{0,3},{1,0},{2,1},{3,2},{4,7},{5,4},{6,5},{7,6},{8,11},{9,8},{10,9... | collective-permute-start | bytes 393224 | tf_op jit(solution)/shard_map/ppermute | solution.py:59
  66.3 1.3 %collective-permute-start.19 = (f32[2,32,256]{2,1,0:T(8,128)S(1)}, f32[2,32,256]{2,1,0:T(8,128)S(1)}, u32[]{:S(2)}, u32[]{:S(2)}) collective-permute-start(f32[2,32,256]{2,1,0:T(8,128)S(1)} %add_add_fusion.2), channel_id=1, source_target_pairs={{0,8},{1,9},{2,10},{3,11},{8,0},{9,1},{10,2},{11,3},{16,24},{17,25... | collective-permute-start | bytes 196616 | tf_op jit(solution)/shard_map/ppermute | solution.py:34
  67.7 11.9 %collective-permute-start.20 = (f32[2,32,256]{2,1,0:T(8,128)S(1)}, f32[2,32,256]{2,1,0:T(8,128)S(1)}, u32[]{:S(2)}, u32[]{:S(2)}) collective-permute-start(f32[2,32,256]{2,1,0:T(8,128)S(1)} %add.142), channel_id=1, source_target_pairs={{0,16},{1,17},{2,18},{3,19},{8,24},{9,25},{10,26},{11,27},{16,0},{... | collective-permute-start | bytes 196616 | tf_op jit(solution)/shard_map/ppermute | solution.py:34
  69.0 10.5 %collective-permute-start.21 = (f32[2,32,256]{2,1,0:T(8,128)S(1)}, f32[2,32,256]{2,1,0:T(8,128)S(1)}, u32[]{:S(2)}, u32[]{:S(2)}) collective-permute-start(f32[2,32,256]{2,1,0:T(8,128)S(1)} %add.142), channel_id=1, source_target_pairs={{0,32},{1,33},{2,34},{3,35},{8,40},{9,41},{10,42},{11,43},{16,48},... | collective-permute-start | bytes 196616 | tf_op jit(solution)/shard_map/ppermute | solution.py:34
  72.8 6.8 %collective-permute-start.22 = (f32[2,32,256]{2,1,0:T(8,128)S(1)}, f32[2,32,256]{2,1,0:T(8,128)S(1)}, u32[]{:S(2)}, u32[]{:S(2)}) collective-permute-start(f32[2,32,256]{2,1,0:T(8,128)S(1)} %add.142), channel_id=1, source_target_pairs={{0,48},{1,49},{2,50},{3,51},{8,56},{9,57},{10,58},{11,59},{16,32},... | collective-permute-start | bytes 196616 | tf_op jit(solution)/shard_map/ppermute | solution.py:34
  74.0 9.4 %collective-permute-start.15 = (bf16[4,128,128]{2,1,0:T(8,128)(2,1)S(1)}, bf16[4,128,128]{2,1,0:T(8,128)(2,1)S(1)}, u32[]{:S(2)}, u32[]{:S(2)}) collective-permute-start(bf16[4,128,128]{2,1,0:T(8,128)(2,1)S(1)} %add_convert_fusion.mine), channel_id=1, source_target_pairs={{0,4},{4,0},{1,5},{5,1},{2,6},{6,2},{3,7},{7,3},{8,12},{12,8},{9,1... | collective-permute-start | bytes 393224 | tf_op jit(solution)/shard_map/ppermute | solution.py:63
  83.4 8.9 %collective-permute-start.23 = (f32[2,32,256]{2,1,0:T(8,128)S(1)}, f32[2,32,256]{2,1,0:T(8,128)S(1)}, u32[]{:S(2)}, u32[]{:S(2)}) collective-permute-start(f32[2,32,256]{2,1,0:T(8,128)S(1)} %add_add_fusion.1), channel_id=1, source_target_pairs={{0,64},{1,65},{2,66},{3,67},{8,72},{9,73},{10,74},{11,75},{16,80},... | collective-permute-start | bytes 196616 | tf_op jit(solution)/shard_map/ppermute | solution.py:34
  85.4 10.9 %collective-permute-start.24 = (f32[2,32,256]{2,1,0:T(8,128)S(1)}, f32[2,32,256]{2,1,0:T(8,128)S(1)}, u32[]{:S(2)}, u32[]{:S(2)}) collective-permute-start(f32[2,32,256]{2,1,0:T(8,128)S(1)} %add_add_fusion.1), channel_id=1, source_target_pairs={{0,128},{1,129},{2,130},{3,131},{8,136},{9,137},{10,138},{11,139},... | collective-permute-start | bytes 196616 | tf_op jit(solution)/shard_map/ppermute | solution.py:34
  91.5 5.8 %collective-permute-start.25 = (f32[2,32,256]{2,1,0:T(8,128)S(1)}, f32[2,32,256]{2,1,0:T(8,128)S(1)}, u32[]{:S(2)}, u32[]{:S(2)}) collective-permute-start(f32[2,32,256]{2,1,0:T(8,128)S(1)} %add_add_fusion.1), channel_id=1, source_target_pairs={{0,192},{1,193},{2,194},{3,195},{8,200},{9,201},{10,202},{11,203},... | collective-permute-start | bytes 196616 | tf_op jit(solution)/shard_map/ppermute | solution.py:34
  97.7 7.0 %collective-permute-start.26 = (bf16[640,128]{1,0:T(8,128)(2,1)S(1)}, bf16[640,128]{1,0:T(8,128)(2,1)S(1)}, u32[]{:S(2)}, u32[]{:S(2)}) collective-permute-start(bf16[640,128]{1,0:T(8,128)(2,1)S(1)} %finish.1), channel_id=1, source_target_pairs={{0,3},{1,0},{2,1},{3,2},{4,7},{5,4},{6,5},{7,6},{8,11},{9,8},{10,9... | collective-permute-start | bytes 491528 | tf_op jit(solution)/shard_map/ppermute | solution.py:59
  97.7 8.6 %collective-permute-start.27 = (bf16[640,128]{1,0:T(8,128)(2,1)S(1)}, bf16[640,128]{1,0:T(8,128)(2,1)S(1)}, u32[]{:S(2)}, u32[]{:S(2)}) collective-permute-start(bf16[640,128]{1,0:T(8,128)(2,1)S(1)} %finish.1), channel_id=1, source_target_pairs={{0,2},{1,3},{2,0},{3,1},{4,6},{5,7},{6,4},{7,5},{8,10},{9,11},{10,... | collective-permute-start | bytes 491528 | tf_op jit(solution)/shard_map/ppermute | solution.py:59
  98.1 9.9 %collective-permute-start.28 = (bf16[640,128]{1,0:T(8,128)(2,1)S(1)}, bf16[640,128]{1,0:T(8,128)(2,1)S(1)}, u32[]{:S(2)}, u32[]{:S(2)}) collective-permute-start(bf16[640,128]{1,0:T(8,128)(2,1)S(1)} %finish.1), channel_id=1, source_target_pairs={{0,1},{1,2},{2,3},{3,0},{4,5},{5,6},{6,7},{7,4},{8,9},{9,10},{10,1... | collective-permute-start | bytes 491528 | tf_op jit(solution)/shard_map/ppermute | solution.py:59
